TPU v7x, 32 devices: a whole 2x2x4 slice. The times are simulated.
32 devices in a mesh: dp: 16 (over z, y, core), cls: 2 (over x).
Axes of the slice: x: 2, y: 2, z: 4, core: 2. Of those that a mesh axis runs over, the one named last changes fastest.
Arguments:
- features: bfloat16 [2048, 12544], P('dp', 'cls'), may hold values from -6 to 6
- fc_weight: bfloat16 [12544, 512], P('cls'), may hold values from -0.0546875 to 0.0546875
- class_weight: bfloat16 [1024, 512], P('cls'), may hold values from -0.29882812 to 0.29882812
- labels: int32 [2048], P('dp'), may hold values from 0 to 1023
Outputs:
- fc_grad: bfloat16 [12544, 512], P('cls')
- class_grad: bfloat16 [1024, 512], P('cls')
All inputs are finite; a program needn't handle non-finite values.
Results may differ from a plain program's by a relative error of at most 0.024.
Values may be sent and summed in bfloat16 or wider, within the bound.
A program may use at most 64 MiB of HBM per device.

v0:
```python
import math

import jax
import jax.numpy as jnp
from jax import lax
from jax.sharding import PartitionSpec as P

SCALE = 64.0
MARGIN = 0.5
SOFTEN = 0.01
EPSILON = 1e-06


def margin_terms(cosine, is_target):
    sine = jnp.sqrt(1.0 + SOFTEN - cosine * cosine)
    shifted = cosine * math.cos(MARGIN) - sine * math.sin(MARGIN)
    powers = jnp.exp(SCALE * jnp.where(is_target, shifted, cosine))
    slopes = SCALE * jnp.where(is_target, math.cos(MARGIN) + math.sin(MARGIN) * cosine / sine, 1.0)
    return (powers, slopes)


def softmax_grad(powers, totals, slopes, is_target, loss_weight):
    onehot = is_target.astype(jnp.float32)
    return ((powers / totals[:, None] - onehot) * loss_weight * slopes).astype(jnp.bfloat16)


def shards(features, fc_weight, class_weight, labels):
    rows_group = features.shape[0]
    class_count = class_weight.shape[0]
    loss_weight = 1.0 / math.sqrt(rows_group * lax.axis_size("dp"))
    position = lax.axis_index("cls")
    rows_block = features
    raw_embed = lax.psum_scatter(
        jnp.dot(rows_block, fc_weight, preferred_element_type=jnp.float32).astype(jnp.bfloat16),
        "cls",
        scatter_dimension=0,
        tiled=True,
    ).astype(jnp.float32)
    embed_norm = jnp.sqrt(jnp.sum(raw_embed * raw_embed, axis=1, keepdims=True) + EPSILON)
    unit_f = raw_embed / embed_norm
    unit_embed = unit_f.astype(jnp.bfloat16)
    class_f = class_weight.astype(jnp.float32)
    class_norm = jnp.sqrt(jnp.sum(class_f * class_f, axis=1, keepdims=True) + EPSILON)
    class_unit_f = class_f / class_norm
    class_unit = class_unit_f.astype(jnp.bfloat16)
    faces_all = lax.all_gather(unit_embed, "cls", axis=0, tiled=True)
    cosine = lax.dot_general(
        faces_all, class_unit, (((1,), (1,)), ((), ())), preferred_element_type=jnp.float32
    )
    columns = position * class_count + lax.broadcasted_iota(jnp.int32, cosine.shape, 1)
    is_target = columns == labels[:, None]
    powers, slopes = margin_terms(cosine, is_target)
    totals = lax.psum(jnp.sum(powers, axis=1), "cls")
    cos_grad = softmax_grad(powers, totals, slopes, is_target, loss_weight)
    rows_block = cos_grad
    unit_grad = lax.psum_scatter(
        jnp.dot(rows_block, class_unit, preferred_element_type=jnp.float32).astype(jnp.bfloat16),
        "cls",
        scatter_dimension=0,
        tiled=True,
    ).astype(jnp.float32)
    class_part = lax.dot_general(
        cos_grad, faces_all, (((0,), (0,)), ((), ())), preferred_element_type=jnp.float32
    )
    raw_grad = (
        (unit_grad - unit_f * jnp.sum(unit_f * unit_grad, axis=1, keepdims=True)) / embed_norm
    ).astype(jnp.bfloat16)
    rows_block = features
    fc_part = lax.dot_general(
        rows_block,
        lax.all_gather(raw_grad, "cls", axis=0, tiled=True),
        (((0,), (0,)), ((), ())),
        preferred_element_type=jnp.float32,
    )
    fc_total, class_total = lax.psum((fc_part, class_part), "dp")
    fc_out = fc_total.astype(jnp.bfloat16)
    class_grad = (
        class_total - class_unit_f * jnp.sum(class_unit_f * class_total, axis=1, keepdims=True)
    ) / class_norm
    return (fc_out, class_grad.astype(jnp.bfloat16))


def solution(mesh):
    placed = (P("dp", "cls"), P("cls", None), P("cls", None), P("dp"))
    return jax.shard_map(
        shards,
        mesh=mesh,
        in_specs=placed,
        out_specs=(P("cls", None), P("cls", None)),
        check_vma=False,
    )
```

profile of v0, /device:TPU:1, one launch (start us, length us, event | category | flops | bytes accessed | tf_op | source)
XLA Modules:
  0.0 361.6 jit_solution(11764674322963167714)
XLA Ops:
  7.2 0.0 copy-start
  7.2 0.0 copy-start.1
  7.2 0.0 copy-start.3
  7.2 0.0 reduce-scatter.3.cloned.1.call-start
  7.2 1.3 copy-done
  8.6 4.5 %convolution_convert_fusion.1 = bf16[128,512]{1,0:T(8,128)(2,1)} fusion(bf16[128,6272]{1,0:T(8,128)(2,1)S(1)} %copy-done, bf16[6272,512]{1,0:T(8,128)(2,1)} %param.5), kind=kOutput, calls=%fused_computation.4 | convolution fusion | flops 822149120 | bytes 8159232 | tf_op jit(solution)/shard_map/dot_general | solution.py:34
  13.1 0.0 reduce-scatter.3.cloned.1.call-update
  13.1 0.0 reduce-scatter.5.cloned.1.call-start
  13.2 0.0 copy-done.1
  13.2 0.2 fusion
  13.4 12.1 %reduce-scatter.3.cloned.1.call-done = bf16[64,512]{1,0:T(8,128)(2,1)} async-done(((bf16[128,512]{1,0:T(8,128)(2,1)}), bf16[64,512]{1,0:T(8,128)(2,1)}) %reduce-scatter.3.cloned.1.call-update) | async-done | bytes 65552 | tf_op jit(solution)/shard_map/reduce_scatter | solution.py:33
  25.5 1.0 fusion.12
  26.5 0.9 fusion.16
  27.4 3.8 %all_gather.6 = bf16[128,512]{1,0:T(8,128)(2,1)S(1)} all-gather(bf16[64,512]{1,0:T(8,128)(2,1)S(1)} %fusion.16), channel_id=1, replica_groups=mesh['dp'=16,'cls'=2] {'cls'}, dimensions={0}, use_global_device_ids=true | all-gather | bytes 196608 | tf_op jit(solution)/shard_map/all_gather | solution.py:46
  31.2 0.0 copy-done.3
  31.2 0.6 fusion.11
  31.8 0.0 copy-start.2
  31.9 3.9 %psum.21 = f32[128]{0:T(128)S(1)} all-reduce(f32[128]{0:T(128)S(1)} %get-tuple-element.4), channel_id=1, replica_groups=mesh['dp'=16,'cls'=2] {'cls'}, use_global_device_ids=true, to_apply=%region_4.5 | all-reduce | flops 128 | bytes 1024 | tf_op jit(solution)/shard_map/psum | solution.py:53
  35.8 1.2 convolution_convert_fusion
  37.0 0.0 reduce-scatter.5.cloned.1.call-update
  37.0 0.0 all-reduce.3.cloned.1.call-start
  37.0 1.5 fusion.17
  38.5 0.0 all-reduce.3.cloned.1.call-update
  38.6 11.2 %reduce-scatter.5.cloned.1.call-done = bf16[64,512]{1,0:T(8,128)(2,1)} async-done(((bf16[128,512]{1,0:T(8,128)(2,1)}), bf16[64,512]{1,0:T(8,128)(2,1)}) %reduce-scatter.5.cloned.1.call-update) | async-done | bytes 65552 | tf_op jit(solution)/shard_map/reduce_scatter | solution.py:56
  49.7 1.0 fusion.13
  50.7 0.9 fusion.15
  51.7 3.8 %all_gather.7 = bf16[128,512]{1,0:T(8,128)(2,1)S(1)} all-gather(bf16[64,512]{1,0:T(8,128)(2,1)S(1)} %fusion.15), channel_id=1, replica_groups=mesh['dp'=16,'cls'=2] {'cls'}, dimensions={0}, use_global_device_ids=true | all-gather | bytes 196608 | tf_op jit(solution)/shard_map/all_gather | solution.py:71
  55.5 6.5 %convolution_bitcast_fusion = f32[6272,512]{0,1:T(8,128)} fusion(bf16[128,512]{1,0:T(8,128)(2,1)S(1)} %all_gather.7, bf16[128,6272]{1,0:T(8,128)(2,1)S(1)} %copy-done), kind=kOutput, calls=%fused_computation | convolution fusion | flops 822083584 | bytes 14581760 | tf_op jit(solution)/shard_map/dot_general | solution.py:69
  62.0 280.0 %all-reduce.4 = bf16[6272,512]{0,1:T(8,128)(2,1)} all-reduce(f32[6272,512]{0,1:T(8,128)} %convolution_bitcast_fusion), channel_id=1, replica_groups=mesh['dp'=16,'cls'=2] {'dp'}, use_global_device_ids=true, to_apply=%region_7.8 | all-reduce | flops 3211264 | bytes 19267584 | tf_op jit(solution)/shard_map/psum | solution.py:75
  341.9 9.4 %copy.6 = bf16[6272,512]{1,0:T(8,128)(2,1)} copy(bf16[6272,512]{0,1:T(8,128)(2,1)} %all-reduce.4) | data formatting | bytes 12845056
  351.3 1.5 multiply_reduce_fusion
  352.8 2.3 divide_convert_fusion
  (5 shorter events, 0.0 us)
Async XLA Ops:
  7.2 1.4 copy-start
  7.2 6.0 %copy-start.1 = (bf16[512,512]{1,0:T(8,128)(2,1)S(1)}, bf16[512,512]{1,0:T(8,128)(2,1)}, u32[]{:S(2)}) copy-start(bf16[512,512]{1,0:T(8,128)(2,1)} %param.6) | copy-start | bytes 1572868
  7.2 24.0 %copy-start.3 = (s32[128]{0:T(128)S(1)}, s32[128]{0:T(128)}, u32[]{:S(2)}) copy-start(s32[128]{0:T(128)} %param.7) | copy-start | bytes 1540
  7.2 18.3 %reduce-scatter.3.cloned.1.call-start = ((), (), s32[]{:S(2)}) async-start(), calls=%async_computation.2 | async-start | bytes 196608 | tf_op jit(solution)/shard_map/reduce_scatter | solution.py:33
  13.1 36.6 %reduce-scatter.5.cloned.1.call-start = ((), (), s32[]{:S(2)}) async-start(), calls=%async_computation.3 | async-start | bytes 196608 | tf_op jit(solution)/shard_map/reduce_scatter | solution.py:56
  31.8 17.9 %copy-start.2 = (bf16[64,512]{1,0:T(8,128)(2,1)S(1)}, bf16[64,512]{1,0:T(8,128)(2,1)}, u32[]{:S(2)}) copy-start(bf16[64,512]{1,0:T(8,128)(2,1)} %reduce-scatter.3.cloned.1.call-done) | copy-start | bytes 196612
  37.0 314.3 %all-reduce.3.cloned.1.call-start = ((), (), s32[]{:S(2)}) async-start(), calls=%async_computation.4 | async-start | bytes 2097152 | tf_op jit(solution)/shard_map/psum | solution.py:75
Sparse Core Ops, SparseCore 0:
  13.2 12.2 reduce-scatter.2
  37.1 12.5 reduce-scatter.4
  53.2 117.5 all-reduce.2
where the time goes:
time: 362 us
  blocking collectives  291 us (80%)
  waiting for transfers between devices  23.4 us (6%)
  matrix products  14.3 us (4%)
  between operations  13.8 us (4%)
  local copies, waits for them, and re-layouts  10.7 us (3%)
  other arithmetic  7.87 us (2%)
    psum x1, blocking collectives, shards(): fc_total, class_total = lax.psum((fc_part, class_part), 'dp')  280 us
    reduce_scatter x1, waiting for transfers between devices, shards(): lax.psum_scatter(jnp.dot(rows_block, fc_weight, preferred_element_type=jn...  12.1 us
    reduce_scatter x1, waiting for transfers between devices, shards(): lax.psum_scatter(jnp.dot(rows_block, class_unit, preferred_element_type=j...  11.2 us
    unnamed x9, local copies, waits for them, and re-layouts  10.7 us
  transfers between devices with their start and end apart: 3, of which 2 were waited for; matrix products, arithmetic and copies ran while one was open for 5% of the time, Pallas kernels for 0%

commit v1 on v0

--- a/solution.py
+++ b/solution.py
@@ -1,8 +1,11 @@
+import functools
 import math
 
 import jax
 import jax.numpy as jnp
 from jax import lax
+from jax.experimental import pallas as pl
+from jax.experimental.pallas import tpu as pltpu
 from jax.sharding import PartitionSpec as P
 
 SCALE = 64.0
@@ -80,10 +83,423 @@
     return (fc_out, class_grad.astype(jnp.bfloat16))
 
 
+MESH = pl.DeviceIdType.MESH
+LANES = 128
+PLANE = 4
+ROUNDED = jnp.bfloat16
+
+
+def split_rows(blocks, parts):
+    base, more = divmod(blocks, parts)
+    runs, start = [], 0
+    for part in range(parts):
+        size = base + (1 if part < more else 0)
+        runs.append((start * LANES, size * LANES))
+        start += size
+    return runs
+
+
+def kernel(
+    nz, chunks, faces_total,
+    feat_hbm, w_hbm, cw_ref, lab_ref,
+    fc_out, class_out,
+    feat, w, gath, praw, rraw, unit_all, cu, tot_s, tot_r, cosg, cg_all, pgrad, rgrad,
+    rg_all, cpart, cslots, cout, f, sendb, from_left, from_right, slab,
+    load_sem, x_send, x_recv, p_send, p_recv, own_sem, c_send, c_recv,
+    ca_send, ca_recv, cp_send, cp_recv, rs_send, rl_recv, rr_recv,
+    az_send, az_recv, ay_send, ay_recv, ac_send, ac_recv, out_sem,
+):
+    rows, fin = feat.shape
+    classes, dim = cw_ref.shape
+    wide = gath.shape[1]
+    per = (fin // LANES // PLANE) * LANES
+    cq = classes // PLANE
+    cz = cq // nz
+    dp = lax.axis_index("dp")
+    x = lax.axis_index("cls")
+    z, q = dp // PLANE, dp % PLANE
+    y, core = q // 2, q % 2
+    q_y = (1 - y) * 2 + core
+    q_c = y * 2 + 1 - core
+    q_d = (1 - y) * 2 + 1 - core
+    x_dev = {"cls": 1 - x}
+    y_dev = {"dp": z * PLANE + q_y}
+    c_dev = {"dp": z * PLANE + q_c}
+    right = {"dp": jnp.minimum(z + 1, nz - 1) * PLANE + q}
+    left = {"dp": jnp.maximum(z - 1, 0) * PLANE + q}
+    plane = [(q + d) % PLANE for d in range(1, PLANE)]
+    plane_from = [(q + PLANE - d) % PLANE for d in range(1, PLANE)]
+    line = [(z + d) % nz for d in range(1, nz)]
+    line_from = [(z + nz - d) % nz for d in range(1, nz)]
+    pending = []
+
+    def send(cond, make):
+        if cond is None:
+            make().start()
+        else:
+            @pl.when(cond)
+            def _():
+                make().start()
+        pending.append((cond, make))
+
+    def remote(src, dst, s, r, dev):
+        return lambda: pltpu.make_async_remote_copy(
+            src_ref=src(), dst_ref=dst(), send_sem=s(), recv_sem=r(),
+            device_id=dev, device_id_type=MESH,
+        )
+
+    def landed(dst, r):
+        pltpu.make_async_remote_copy(
+            src_ref=dst, dst_ref=dst, send_sem=r, recv_sem=r,
+            device_id=x_dev, device_id_type=MESH,
+        ).wait_recv()
+
+    def at(i, n):
+        return pl.ds(pl.multiple_of(i * n, n), n)
+
+    steps = load_sem.shape[0] // 2
+    kk = fin // steps
+    loads = []
+    for k in range(steps):
+        part = pl.ds(k * kk, kk)
+        pair = (
+            pltpu.make_async_copy(w_hbm.at[part, :], w.at[part, :], load_sem.at[2 * k]),
+            pltpu.make_async_copy(feat_hbm.at[:, part], feat.at[:, part], load_sem.at[2 * k + 1]),
+        )
+        for copy in pair:
+            copy.start()
+        loads.append(pair)
+
+    barrier = pltpu.get_barrier_semaphore()
+    peers = [x_dev] + [{"dp": z * PLANE + p} for p in plane] + [{"dp": t * PLANE + q} for t in line]
+    for dev in peers:
+        pl.semaphore_signal(barrier, inc=1, device_id=dev, device_id_type=MESH)
+    pl.semaphore_wait(barrier, len(peers))
+
+    mine = at(q, rows)
+    own_feat = pltpu.make_async_copy(
+        feat_hbm.at[:, pl.ds(pl.multiple_of(q * per, LANES), wide)], gath.at[mine, :], own_sem.at[0]
+    )
+    own_feat.start()
+    for i, p in enumerate(plane):
+        cols = pl.ds(pl.multiple_of(p * per, LANES), wide)
+        send(None, remote(
+            lambda cols=cols: feat_hbm.at[:, cols], lambda: gath.at[mine, :],
+            lambda i=i: p_send.at[0, i], lambda i=i: p_recv.at[0, i], {"dp": z * PLANE + p},
+        ))
+
+    total = jnp.zeros((rows, dim), jnp.float32)
+    for k in range(steps):
+        for copy in loads[k]:
+            copy.wait()
+        part = pl.ds(k * kk, kk)
+        total = total + jnp.dot(feat[:, part], w[part, :], preferred_element_type=jnp.float32)
+    praw[...] = total.astype(ROUNDED)
+    send(None, remote(lambda: praw, lambda: rraw, lambda: x_send.at[0], lambda: x_recv.at[0], x_dev))
+
+    class_f = cw_ref[...].astype(jnp.float32)
+    class_norm = jnp.sqrt(jnp.sum(class_f * class_f, axis=1, keepdims=True) + EPSILON)
+    cu[...] = (class_f / class_norm).astype(ROUNDED)
+
+    landed(rraw, x_recv.at[0])
+    raw = praw[...].astype(jnp.float32) + rraw[...].astype(jnp.float32)
+    norm = jnp.sqrt(jnp.sum(raw * raw, axis=1, keepdims=True) + EPSILON)
+    unit_f = raw / norm
+    unit = unit_f.astype(ROUNDED)
+    unit_all[mine, :] = unit
+    for i, p in enumerate(plane):
+        send(None, remote(
+            lambda: unit_all.at[mine, :], lambda: unit_all.at[mine, :],
+            lambda i=i: p_send.at[1, i], lambda i=i: p_recv.at[1, i], {"dp": z * PLANE + p},
+        ))
+    cosine = lax.dot_general(
+        unit, cu[...], (((1,), (1,)), ((), ())), preferred_element_type=jnp.float32
+    )
+    columns = x * classes + lax.broadcasted_iota(jnp.int32, cosine.shape, 1)
+    is_target = columns == lab_ref[...]
+    powers, slopes = margin_terms(cosine, is_target)
+    partial = jnp.sum(powers, axis=1, keepdims=True)
+    tot_s[...] = jnp.broadcast_to(partial, tot_s.shape)
+    send(None, remote(lambda: tot_s, lambda: tot_r, lambda: x_send.at[1], lambda: x_recv.at[1], x_dev))
+    landed(tot_r, x_recv.at[1])
+    totals = partial + tot_r[:, 0:1]
+    weight = 1.0 / math.sqrt(faces_total)
+    grad = ((powers / totals - is_target.astype(jnp.float32)) * weight * slopes).astype(ROUNDED)
+    cosg[...] = grad
+    pgrad[...] = jnp.dot(grad, cu[...], preferred_element_type=jnp.float32).astype(ROUNDED)
+    send(None, remote(lambda: pgrad, lambda: rgrad, lambda: x_send.at[2], lambda: x_recv.at[2], x_dev))
+    for i, p in enumerate(plane):
+        cols = at(p, cq)
+        send(None, remote(
+            lambda cols=cols: cosg.at[:, cols], lambda: cg_all.at[mine, :],
+            lambda i=i: p_send.at[2, i], lambda i=i: p_recv.at[2, i], {"dp": z * PLANE + p},
+        ))
+    cg_all[mine, :] = cosg[:, at(q, cq)]
+
+    landed(rgrad, x_recv.at[2])
+    unit_grad = pgrad[...].astype(jnp.float32) + rgrad[...].astype(jnp.float32)
+    along = jnp.sum(unit_f * unit_grad, axis=1, keepdims=True)
+    rg_all[mine, :] = ((unit_grad - unit_f * along) / norm).astype(ROUNDED)
+    for i, p in enumerate(plane):
+        send(None, remote(
+            lambda: rg_all.at[mine, :], lambda: rg_all.at[mine, :],
+            lambda i=i: p_send.at[3, i], lambda i=i: p_recv.at[3, i], {"dp": z * PLANE + p},
+        ))
+
+    for i, p in enumerate(plane_from):
+        theirs = at(p, rows)
+        landed(unit_all.at[theirs, :], p_recv.at[1, i])
+        landed(cg_all.at[theirs, :], p_recv.at[2, i])
+    cpart[...] = lax.dot_general(
+        cg_all[...], unit_all[...], (((0,), (0,)), ((), ())), preferred_element_type=jnp.float32
+    )
+    for i, t in enumerate(line):
+        send(None, remote(
+            lambda t=t: cpart.at[at(t, cz), :], lambda: cslots.at[z],
+            lambda i=i: c_send.at[i], lambda i=i: c_recv.at[i], {"dp": t * PLANE + q},
+        ))
+
+    own_feat.wait()
+    for i, p in enumerate(plane_from):
+        theirs = at(p, rows)
+        landed(gath.at[theirs, :], p_recv.at[0, i])
+        landed(rg_all.at[theirs, :], p_recv.at[3, i])
+
+    def multiply(c):
+        first, size = chunks[c]
+        part = pl.ds(first, size)
+        product = lax.dot_general(
+            gath[:, part], rg_all[...], (((0,), (0,)), ((), ())), preferred_element_type=jnp.float32
+        )
+        for j in range(nz):
+            f[j, part, :] = product[:, j * LANES:(j + 1) * LANES]
+
+    def reduce(c):
+        first, size = chunks[c]
+        part = pl.ds(first, size)
+
+        def pass_on(j, going, starts, arrived, sem, dev, way):
+            @pl.when(jnp.logical_and(going, starts))
+            def _():
+                sendb[j, part, :] = f[j, part, :].astype(ROUNDED)
+
+            @pl.when(jnp.logical_and(going, jnp.logical_not(starts)))
+            def _():
+                landed(arrived.at[j, part, :], sem.at[c, j])
+                sendb[j, part, :] = (
+                    f[j, part, :] + arrived[j, part, :].astype(jnp.float32)
+                ).astype(ROUNDED)
+
+            send(going, remote(
+                lambda: sendb.at[j, part, :], lambda: arrived.at[j, part, :],
+                lambda: rs_send.at[c, j], lambda: sem.at[c, j], dev,
+            ))
+
+        for i in range(nz - 1):
+            j = nz - 1 - i
+            pass_on(j, z < j, z == 0, from_left, rl_recv, right, 0)
+            pass_on(i, z > i, z == nz - 1, from_right, rr_recv, left, 1)
+
+        @pl.when(z > 0)
+        def _():
+            landed(from_left.at[z, part, :], rl_recv.at[c, z])
+            f[z, part, :] += from_left[z, part, :].astype(jnp.float32)
+
+        @pl.when(z < nz - 1)
+        def _():
+            landed(from_right.at[z, part, :], rr_recv.at[c, z])
+            f[z, part, :] += from_right[z, part, :].astype(jnp.float32)
+
+        slab[q, z, part, :] = f[z, part, :].astype(ROUNDED)
+        spread(c, z, z < nz - 1, z > 0, None)
+
+    def spread(c, s, to_right, to_left, there):
+        first, size = chunks[c]
+        part = pl.ds(first, size)
+        block = lambda: slab.at[q, s, part, :]
+        if to_right is not None:
+            send(to_right, remote(block, block, lambda: az_send.at[c, s, 0], lambda: az_recv.at[c, s], right))
+        if to_left is not None:
+            send(to_left, remote(block, block, lambda: az_send.at[c, s, 1], lambda: az_recv.at[c, s], left))
+        send(there, remote(block, block, lambda: ay_send.at[c, s], lambda: ay_recv.at[c, s], y_dev))
+        send(there, remote(block, block, lambda: ac_send.at[0, c, s], lambda: ac_recv.at[0, c, s], c_dev))
+
+    def gather_line(c):
+        first, size = chunks[c]
+        part = pl.ds(first, size)
+        for d in range(1, nz):
+            low, high = jnp.maximum(z - d, 0), jnp.minimum(z + d, nz - 1)
+            has_low, has_high = z >= d, z + d < nz
+
+            @pl.when(has_low)
+            def _():
+                landed(slab.at[q, low, part, :], az_recv.at[c, low])
+
+            spread(c, low, jnp.logical_and(has_low, z < nz - 1), None, has_low)
+
+            @pl.when(has_high)
+            def _():
+                landed(slab.at[q, high, part, :], az_recv.at[c, high])
+
+            spread(c, high, None, jnp.logical_and(has_high, z > 0), has_high)
+
+    def gather_across(c):
+        first, size = chunks[c]
+        part = pl.ds(first, size)
+        for d in range(nz):
+            s = (z + d) % nz
+            landed(slab.at[q_y, s, part, :], ay_recv.at[c, s])
+            block = lambda s=s: slab.at[q_y, s, part, :]
+            send(None, remote(
+                block, block, lambda s=s: ac_send.at[1, c, s], lambda s=s: ac_recv.at[1, c, s], c_dev,
+            ))
+
+    def class_rows():
+        for i, t in enumerate(line_from):
+            landed(cslots.at[t], c_recv.at[i])
+        here = pl.ds(pl.multiple_of(q * cq + z * cz, cz), cz)
+        sums = cpart[at(z, cz), :]
+        for i, t in enumerate(line_from):
+            sums = sums + cslots[t]
+        mine_f = cw_ref[here, :].astype(jnp.float32)
+        mine_norm = jnp.sqrt(jnp.sum(mine_f * mine_f, axis=1, keepdims=True) + EPSILON)
+        mine_unit = mine_f / mine_norm
+        along = jnp.sum(mine_unit * sums, axis=1, keepdims=True)
+        cout[here, :] = ((sums - mine_unit * along) / mine_norm).astype(ROUNDED)
+        for i, t in enumerate(line):
+            send(None, remote(
+                lambda: cout.at[here, :], lambda: cout.at[here, :],
+                lambda i=i: ca_send.at[i], lambda i=i: ca_recv.at[i], {"dp": t * PLANE + q},
+            ))
+
+    def class_plane():
+        for i, t in enumerate(line_from):
+            there = pl.ds(pl.multiple_of(q * cq + t * cz, cz), cz)
+            landed(cout.at[there, :], ca_recv.at[i])
+        block = lambda: cout.at[at(q, cq), :]
+        send(None, remote(block, block, lambda: cp_send.at[0], lambda: cp_recv.at[0], y_dev))
+        send(None, remote(block, block, lambda: cp_send.at[1], lambda: cp_recv.at[1], c_dev))
+
+    def class_across():
+        landed(cout.at[at(q_y, cq), :], cp_recv.at[0])
+        block = lambda: cout.at[at(q_y, cq), :]
+        send(None, remote(block, block, lambda: cp_send.at[2], lambda: cp_recv.at[2], c_dev))
+
+    count = len(chunks)
+    for step in range(count + 2):
+        if step < count:
+            multiply(step)
+            reduce(step)
+        if step == 0:
+            class_rows()
+        if 1 <= step <= count:
+            gather_line(step - 1)
+        if step == 1:
+            class_plane()
+        if step >= 2:
+            gather_across(step - 2)
+        if step == 2:
+            class_across()
+
+    for c in range(count):
+        part = pl.ds(*chunks[c])
+        for s in range(nz):
+            landed(slab.at[q_c, s, part, :], ac_recv.at[0, c, s])
+            landed(slab.at[q_d, s, part, :], ac_recv.at[1, c, s])
+    copies = []
+    for p in range(PLANE):
+        size = wide if p == PLANE - 1 else per
+        for j in range(nz):
+            copies.append(pltpu.make_async_copy(
+                slab.at[p, j, pl.ds(0, size), :],
+                fc_out.at[pl.ds(p * per, size), pl.ds(j * LANES, LANES)],
+                out_sem.at[p * nz + j],
+            ))
+    for copy in copies:
+        copy.start()
+    landed(cout.at[at(q_c, cq), :], cp_recv.at[1])
+    landed(cout.at[at(q_d, cq), :], cp_recv.at[2])
+    class_out[...] = cout[...]
+    for cond, make in pending:
+        if cond is None:
+            make().wait_send()
+        else:
+            @pl.when(cond)
+            def _():
+                make().wait_send()
+    for copy in copies:
+        copy.wait()
+
+
+def fused(n_dp, features, fc_weight, class_weight, labels):
+    rows, fin = features.shape
+    classes, dim = class_weight.shape
+    nz = n_dp // PLANE
+    blocks = fin // LANES
+    wide = (blocks - (PLANE - 1) * (blocks // PLANE)) * LANES
+    chunks = split_rows(wide // LANES, min(4, wide // LANES))
+    count = len(chunks)
+    steps = max(d for d in range(1, 9) if blocks % d == 0)
+    bf, f32, dma = jnp.bfloat16, jnp.float32, pltpu.SemaphoreType.DMA
+    vmem, whole = pltpu.VMEM, pl.BlockSpec(memory_space=pltpu.VMEM)
+    anywhere = pl.BlockSpec(memory_space=pl.ANY)
+    return pl.pallas_call(
+        functools.partial(kernel, nz, chunks, rows * n_dp),
+        out_shape=(
+            jax.ShapeDtypeStruct((fin, dim), bf),
+            jax.ShapeDtypeStruct((classes, dim), bf),
+        ),
+        in_specs=[anywhere, anywhere, whole, whole],
+        out_specs=(anywhere, whole),
+        scratch_shapes=[
+            vmem((rows, fin), bf), vmem((fin, dim), bf), vmem((PLANE * rows, wide), bf),
+            vmem((rows, dim), bf), vmem((rows, dim), bf), vmem((PLANE * rows, dim), bf),
+            vmem((classes, dim), bf), vmem((rows, LANES), f32), vmem((rows, LANES), f32),
+            vmem((rows, classes), bf), vmem((PLANE * rows, classes // PLANE), bf),
+            vmem((rows, dim), bf), vmem((rows, dim), bf), vmem((PLANE * rows, dim), bf),
+            vmem((classes // PLANE, dim), f32), vmem((nz, classes // PLANE // nz, dim), f32),
+            vmem((classes, dim), bf), vmem((nz, wide, LANES), f32),
+            vmem((nz, wide, LANES), bf), vmem((nz, wide, LANES), bf), vmem((nz, wide, LANES), bf),
+            vmem((PLANE, nz, wide, LANES), bf),
+            dma((2 * steps,)), dma((3,)), dma((3,)), dma((4, PLANE - 1)), dma((4, PLANE - 1)),
+            dma((1,)), dma((nz - 1,)), dma((nz - 1,)), dma((nz - 1,)), dma((nz - 1,)),
+            dma((3,)), dma((3,)), dma((count, nz)), dma((count, nz)), dma((count, nz)),
+            dma((count, nz, 2)), dma((count, nz)), dma((count, nz)), dma((count, nz)),
+            dma((2, count, nz)), dma((2, count, nz)), dma((PLANE * nz,)),
+        ],
+        compiler_params=pltpu.CompilerParams(
+            collective_id=0, has_side_effects=True, vmem_limit_bytes=52 * 2**20
+        ),
+    )(features, fc_weight, class_weight, labels.reshape(rows, 1))
+
+
+def choose(n_dp, n_cls, features, fc_weight, class_weight, labels):
+    rows, fin = features.shape
+    classes, dim = class_weight.shape
+    nz = n_dp // PLANE
+    fits = (
+        n_cls == 2
+        and n_dp % PLANE == 0
+        and nz > 1
+        and dim == nz * LANES
+        and fin % LANES == 0
+        and fin // LANES >= PLANE
+        and rows % 16 == 0
+        and rows <= 128
+        and classes % (PLANE * LANES) == 0
+        and classes // PLANE % (16 * nz) == 0
+        and classes <= 512
+        and fin <= 6272
+    )
+    if fits:
+        return fused(n_dp, features, fc_weight, class_weight, labels)
+    return shards(features, fc_weight, class_weight, labels)
+
+
 def solution(mesh):
     placed = (P("dp", "cls"), P("cls", None), P("cls", None), P("dp"))
     return jax.shard_map(
-        shards,
+        functools.partial(choose, mesh.shape["dp"], mesh.shape["cls"]),
         mesh=mesh,
         in_specs=placed,
         out_specs=(P("cls", None), P("cls", None)),

time: 362 us -> 158 us (0.44)
  blocking collectives: 291 us -> 0 us
  Pallas kernels: 0 us -> 148 us
  waiting for transfers between devices: 23.4 us -> 0 us
  matrix products: 14.3 us -> 0 us
  between operations: 13.8 us -> 0.64 us
  other arithmetic: 7.87 us -> 0 us
    psum x2 -> x0, blocking collectives: 284 us -> none  [the longest x1 280 us: shards(): fc_total, class_total = lax.psum((fc_part, class_part), 'dp')]
    pallas_call x0 -> x1, Pallas kernels: none -> 148 us  [fused(): pl.pallas_call(functools.partial(kernel, nz, chunks, rows * n_dp), out_sh...]
    reduce_scatter x2 -> x0, waiting for transfers between devices: 23.3 us -> none  [the longest x1 12.1 us: shards(): lax.psum_scatter(jnp.dot(rows_block, fc_weight, preferred_element_type=jn...]
    dot_general x5 -> x0, matrix products: 14.3 us -> none  [the longest x1 6.47 us: shards(): lax.dot_general(rows_block, lax.all_gather(raw_grad, 'cls', axis=0, tiled...]
    all_gather x2 -> x0, blocking collectives: 7.59 us -> none  [the longest x1 3.79 us: shards(): faces_all = lax.all_gather(unit_embed, 'cls', axis=0, tiled=True)]
    convert_element_type x3 -> x0, other arithmetic: 4.18 us -> none  [the longest x1 2.3 us: shards(): return (fc_out, class_grad.astype(jnp.bfloat16))]
    reduce_sum x4 -> x0, other arithmetic: 3.68 us -> none  [the longest x1 1.51 us: shards(): jnp.sum(class_unit_f * class_total, axis=1, keepdims=True)]
    unnamed x9 -> x4, local copies, waits for them, and re-layouts: 10.7 us -> 7.81 us
  transfers between devices with their start and end apart: 3 -> 0, of which waited for: 2 -> 0; matrix products, arithmetic and copies ran while one was open for 5% -> 0% of each run, Pallas kernels for 0% -> 0%
where the time goes in v1:
time: 158 us
  Pallas kernels  148 us (94%)
  local copies, waits for them, and re-layouts  8.57 us (5%)
    pallas_call x1, Pallas kernels, fused(): pl.pallas_call(functools.partial(kernel, nz, chunks, rows * n_dp), out_sh...  148 us
    unnamed x4, local copies, waits for them, and re-layouts  7.81 us

profile of v1, /device:TPU:1, one launch (start us, length us, event | category | flops | bytes accessed | tf_op | source)
XLA Modules:
  0.0 157.7 jit_solution(4657294421967438484)
XLA Ops:
  0.6 0.8 copy.6.lab_ref
  1.4 0.0 copy-start
  1.4 1.0 copy-done
  2.4 148.5 %shard_map.59 = (bf16[6272,512]{1,0:T(8,128)(2,1)}, bf16[512,512]{1,0:T(8,128)(2,1)S(1)}) custom-call(bf16[128,6272]{1,0:T(8,128)(2,1)} %feat_hbm.1, bf16[6272,512]{1,0:T(8,128)(2,1)} %w_hbm.1, bf16[512,512]{1,0:T(8,128)(2,1)S(1)} %copy-done, s32[128,1]{1,0:T(8,128)S(1)} %copy.6.lab_ref), custom_call_target="tpu_custom_call" | custom-call | tf_op jit(solution)/shard_map/pallas_call | solution.py:446
  150.9 6.0 %copy.9 = bf16[6272,512]{1,0:T(8,128)(2,1)} copy(bf16[6272,512]{1,0:T(8,128)(2,1)} %get-tuple-element.4) | data formatting | bytes 12845056
  156.9 0.8 copy.10
Async XLA Ops:
  1.4 1.0 copy-start

commit v2 on v1

--- a/solution.py
+++ b/solution.py
@@ -101,13 +101,12 @@
 
 def kernel(
     nz, chunks, faces_total,
-    feat_hbm, w_hbm, cw_ref, lab_ref,
-    fc_out, class_out,
-    feat, w, gath, praw, rraw, unit_all, cu, tot_s, tot_r, cosg, cg_all, pgrad, rgrad,
-    rg_all, cpart, cslots, cout, f, sendb, from_left, from_right, slab,
+    feat_hbm, w_hbm, cw_hbm, lab_hbm,
+    fc_out, cout,
+    slab, feat, w, cw_ref, lab_ref, gath, praw, rraw, unit_all, cu, tot_s, tot_r, cosg, cg_all, pgrad, rgrad,
+    rg_all, cpart, cslots, f, send1, recv1, send2, recv2,
     load_sem, x_send, x_recv, p_send, p_recv, own_sem, c_send, c_recv,
-    ca_send, ca_recv, cp_send, cp_recv, rs_send, rl_recv, rr_recv,
-    az_send, az_recv, ay_send, ay_recv, ac_send, ac_recv, out_sem,
+    ca_send, ca_recv, cp_send, cp_recv, z_send, z_recv, y_send, y_recv, n_send, n_recv, out_sem,
 ):
     rows, fin = feat.shape
     classes, dim = cw_ref.shape
@@ -125,8 +124,10 @@
     x_dev = {"cls": 1 - x}
     y_dev = {"dp": z * PLANE + q_y}
     c_dev = {"dp": z * PLANE + q_c}
-    right = {"dp": jnp.minimum(z + 1, nz - 1) * PLANE + q}
-    left = {"dp": jnp.maximum(z - 1, 0) * PLANE + q}
+    half, side = z // 2, z % 2
+    near = {"dp": (half * 2 + 1 - side) * PLANE + q}
+    far = {"dp": ((1 - half) * 2 + side) * PLANE + q}
+    owned = side * 2 + half
     plane = [(q + d) % PLANE for d in range(1, PLANE)]
     plane_from = [(q + PLANE - d) % PLANE for d in range(1, PLANE)]
     line = [(z + d) % nz for d in range(1, nz)]
@@ -157,6 +158,12 @@
     def at(i, n):
         return pl.ds(pl.multiple_of(i * n, n), n)
 
+    small = [
+        pltpu.make_async_copy(cw_hbm, cw_ref, own_sem.at[1]),
+        pltpu.make_async_copy(lab_hbm, lab_ref, own_sem.at[2]),
+    ]
+    for copy in small:
+        copy.start()
     steps = load_sem.shape[0] // 2
     kk = fin // steps
     loads = []
@@ -197,6 +204,8 @@
     praw[...] = total.astype(ROUNDED)
     send(None, remote(lambda: praw, lambda: rraw, lambda: x_send.at[0], lambda: x_recv.at[0], x_dev))
 
+    for copy in small:
+        copy.wait()
     class_f = cw_ref[...].astype(jnp.float32)
     class_norm = jnp.sqrt(jnp.sum(class_f * class_f, axis=1, keepdims=True) + EPSILON)
     cu[...] = (class_f / class_norm).astype(ROUNDED)
@@ -216,7 +225,8 @@
         unit, cu[...], (((1,), (1,)), ((), ())), preferred_element_type=jnp.float32
     )
     columns = x * classes + lax.broadcasted_iota(jnp.int32, cosine.shape, 1)
-    is_target = columns == lab_ref[...]
+    label = jnp.broadcast_to(lab_ref[...], (LANES, rows)).T[:, 0:1]
+    is_target = columns == label
     powers, slopes = margin_terms(cosine, is_target)
     partial = jnp.sum(powers, axis=1, keepdims=True)
     tot_s[...] = jnp.broadcast_to(partial, tot_s.shape)
@@ -265,94 +275,81 @@
         landed(gath.at[theirs, :], p_recv.at[0, i])
         landed(rg_all.at[theirs, :], p_recv.at[3, i])
 
-    def multiply(c):
-        first, size = chunks[c]
-        part = pl.ds(first, size)
+    count = len(chunks)
+    split = max(count - 3, 0)
+    writes = []
+
+    def exchange(src, dst, sends, recvs, dev, *spot):
+        send(None, remote(
+            lambda: src, lambda: dst, lambda: sends.at[spot], lambda: recvs.at[spot], dev,
+        ))
+
+    def pair(p, which, part):
+        return slab.at[p, pl.ds(which * 2, 2), part, :]
+
+    def multiply(c, part):
         product = lax.dot_general(
             gath[:, part], rg_all[...], (((0,), (0,)), ((), ())), preferred_element_type=jnp.float32
         )
         for j in range(nz):
             f[j, part, :] = product[:, j * LANES:(j + 1) * LANES]
-
-    def reduce(c):
-        first, size = chunks[c]
-        part = pl.ds(first, size)
-
-        def pass_on(j, going, starts, arrived, sem, dev, way):
-            @pl.when(jnp.logical_and(going, starts))
-            def _():
-                sendb[j, part, :] = f[j, part, :].astype(ROUNDED)
-
-            @pl.when(jnp.logical_and(going, jnp.logical_not(starts)))
-            def _():
-                landed(arrived.at[j, part, :], sem.at[c, j])
-                sendb[j, part, :] = (
-                    f[j, part, :] + arrived[j, part, :].astype(jnp.float32)
-                ).astype(ROUNDED)
-
-            send(going, remote(
-                lambda: sendb.at[j, part, :], lambda: arrived.at[j, part, :],
-                lambda: rs_send.at[c, j], lambda: sem.at[c, j], dev,
-            ))
-
-        for i in range(nz - 1):
-            j = nz - 1 - i
-            pass_on(j, z < j, z == 0, from_left, rl_recv, right, 0)
-            pass_on(i, z > i, z == nz - 1, from_right, rr_recv, left, 1)
-
-        @pl.when(z > 0)
-        def _():
-            landed(from_left.at[z, part, :], rl_recv.at[c, z])
-            f[z, part, :] += from_left[z, part, :].astype(jnp.float32)
-
-        @pl.when(z < nz - 1)
-        def _():
-            landed(from_right.at[z, part, :], rr_recv.at[c, z])
-            f[z, part, :] += from_right[z, part, :].astype(jnp.float32)
-
-        slab[q, z, part, :] = f[z, part, :].astype(ROUNDED)
-        spread(c, z, z < nz - 1, z > 0, None)
-
-    def spread(c, s, to_right, to_left, there):
-        first, size = chunks[c]
-        part = pl.ds(first, size)
-        block = lambda: slab.at[q, s, part, :]
-        if to_right is not None:
-            send(to_right, remote(block, block, lambda: az_send.at[c, s, 0], lambda: az_recv.at[c, s], right))
-        if to_left is not None:
-            send(to_left, remote(block, block, lambda: az_send.at[c, s, 1], lambda: az_recv.at[c, s], left))
-        send(there, remote(block, block, lambda: ay_send.at[c, s], lambda: ay_recv.at[c, s], y_dev))
-        send(there, remote(block, block, lambda: ac_send.at[0, c, s], lambda: ac_recv.at[0, c, s], c_dev))
-
-    def gather_line(c):
-        first, size = chunks[c]
-        part = pl.ds(first, size)
-        for d in range(1, nz):
-            low, high = jnp.maximum(z - d, 0), jnp.minimum(z + d, nz - 1)
-            has_low, has_high = z >= d, z + d < nz
-
-            @pl.when(has_low)
-            def _():
-                landed(slab.at[q, low, part, :], az_recv.at[c, low])
-
-            spread(c, low, jnp.logical_and(has_low, z < nz - 1), None, has_low)
-
-            @pl.when(has_high)
-            def _():
-                landed(slab.at[q, high, part, :], az_recv.at[c, high])
-
-            spread(c, high, None, jnp.logical_and(has_high, z > 0), has_high)
-
-    def gather_across(c):
-        first, size = chunks[c]
-        part = pl.ds(first, size)
-        for d in range(nz):
-            s = (z + d) % nz
-            landed(slab.at[q_y, s, part, :], ay_recv.at[c, s])
-            block = lambda s=s: slab.at[q_y, s, part, :]
-            send(None, remote(
-                block, block, lambda s=s: ac_send.at[1, c, s], lambda s=s: ac_recv.at[1, c, s], c_dev,
-            ))
+        for i in range(2):
+            send1[i, part, :] = f[(1 - side) * 2 + i, part, :].astype(ROUNDED)
+        exchange(send1.at[:, part, :], recv1.at[:, part, :], z_send, z_recv, near, 0, c)
+
+    def sum_near(c, part):
+        landed(recv1.at[:, part, :], z_recv.at[0, c])
+        send2[part, :] = (
+            f[side * 2 + 1 - half, part, :] + recv1[1 - half, part, :].astype(jnp.float32)
+        ).astype(ROUNDED)
+        exchange(send2.at[part, :], recv2.at[part, :], z_send, z_recv, far, 1, c)
+
+    def sum_far(c, part):
+        landed(recv2.at[part, :], z_recv.at[1, c])
+        slab[q, owned, part, :] = (
+            f[owned, part, :]
+            + recv1[half, part, :].astype(jnp.float32)
+            + recv2[part, :].astype(jnp.float32)
+        ).astype(ROUNDED)
+        block = slab.at[q, owned, part, :]
+        exchange(block, block, z_send, z_recv, far, 2, c)
+
+    def gather_far(c, part):
+        landed(slab.at[q, side * 2 + 1 - half, part, :], z_recv.at[2, c])
+        block = pair(q, side, part)
+        exchange(block, block, z_send, z_recv, near, 3, c)
+        exchange(block, block, y_send, y_recv, y_dev, side, c)
+        exchange(block, block, n_send, n_recv, c_dev, side, c)
+
+    def gather_near(c, part):
+        block = pair(q, 1 - side, part)
+        landed(block, z_recv.at[3, c])
+        exchange(block, block, y_send, y_recv, y_dev, 1 - side, c)
+        exchange(block, block, n_send, n_recv, c_dev, 1 - side, c)
+
+    def gather_across(c, part):
+        for which in (side, 1 - side):
+            block = pair(q_y, which, part)
+            landed(block, y_recv.at[which, c])
+            exchange(block, block, n_send, n_recv, c_dev, 2 + which, c)
+
+    def gather_core(c, part):
+        for which in range(2):
+            landed(pair(q_c, which, part), n_recv.at[which, c])
+            landed(pair(q_d, which, part), n_recv.at[2 + which, c])
+        if c in (split, count - 1):
+            low = 0 if c == split else chunks[split + 1][0]
+            high = part.start + part.size
+            for p in range(PLANE):
+                size = (high if p == PLANE - 1 else min(high, per)) - low
+                for j in range(nz):
+                    copy = pltpu.make_async_copy(
+                        slab.at[p, j, pl.ds(low, size), :],
+                        fc_out.at[pl.ds(p * per + low, size), pl.ds(j * LANES, LANES)],
+                        out_sem.at[int(c != split), p * nz + j],
+                    )
+                    copy.start()
+                    writes.append(copy)
 
     def class_rows():
         for i, t in enumerate(line_from):
@@ -385,48 +382,36 @@
         block = lambda: cout.at[at(q_y, cq), :]
         send(None, remote(block, block, lambda: cp_send.at[2], lambda: cp_recv.at[2], c_dev))
 
-    count = len(chunks)
-    for step in range(count + 2):
-        if step < count:
-            multiply(step)
-            reduce(step)
-        if step == 0:
+    stages = (multiply, sum_near, sum_far, gather_far, gather_near, gather_across, gather_core)
+    for tick in range(count + len(stages) - 1):
+        for stage, run in enumerate(stages):
+            c = tick - stage
+            if 0 <= c < count:
+                run(c, pl.ds(*chunks[c]))
+        if tick == 1:
             class_rows()
-        if 1 <= step <= count:
-            gather_line(step - 1)
-        if step == 1:
+        if tick == 2:
             class_plane()
-        if step >= 2:
-            gather_across(step - 2)
-        if step == 2:
+        if tick == 3:
             class_across()
 
-    for c in range(count):
-        part = pl.ds(*chunks[c])
-        for s in range(nz):
-            landed(slab.at[q_c, s, part, :], ac_recv.at[0, c, s])
-            landed(slab.at[q_d, s, part, :], ac_recv.at[1, c, s])
-    copies = []
-    for p in range(PLANE):
-        size = wide if p == PLANE - 1 else per
-        for j in range(nz):
-            copies.append(pltpu.make_async_copy(
-                slab.at[p, j, pl.ds(0, size), :],
-                fc_out.at[pl.ds(p * per, size), pl.ds(j * LANES, LANES)],
-                out_sem.at[p * nz + j],
-            ))
+    landed(cout.at[at(q_c, cq), :], cp_recv.at[1])
+    landed(cout.at[at(q_d, cq), :], cp_recv.at[2])
+    for cond, make in pending:
+        make().wait_send()
+    for copy in writes:
+        copy.wait()
+
+
+def place(fc_in, class_in, fc_out, class_out, sems):
+    pieces = sems.shape[0] - 1
+    size = fc_in.shape[0] // pieces
+    copies = [pltpu.make_async_copy(class_in, class_out, sems.at[pieces])]
+    for i in range(pieces):
+        part = pl.ds(i * size, size)
+        copies.append(pltpu.make_async_copy(fc_in.at[part, :], fc_out.at[part, :], sems.at[i]))
     for copy in copies:
         copy.start()
-    landed(cout.at[at(q_c, cq), :], cp_recv.at[1])
-    landed(cout.at[at(q_d, cq), :], cp_recv.at[2])
-    class_out[...] = cout[...]
-    for cond, make in pending:
-        if cond is None:
-            make().wait_send()
-        else:
-            @pl.when(cond)
-            def _():
-                make().wait_send()
     for copy in copies:
         copy.wait()
 
@@ -437,40 +422,51 @@
     nz = n_dp // PLANE
     blocks = fin // LANES
     wide = (blocks - (PLANE - 1) * (blocks // PLANE)) * LANES
-    chunks = split_rows(wide // LANES, min(4, wide // LANES))
+    chunks = split_rows(wide // LANES, min(7, wide // LANES))
     count = len(chunks)
     steps = max(d for d in range(1, 9) if blocks % d == 0)
     bf, f32, dma = jnp.bfloat16, jnp.float32, pltpu.SemaphoreType.DMA
     vmem, whole = pltpu.VMEM, pl.BlockSpec(memory_space=pltpu.VMEM)
     anywhere = pl.BlockSpec(memory_space=pl.ANY)
-    return pl.pallas_call(
+    results = pl.pallas_call(
         functools.partial(kernel, nz, chunks, rows * n_dp),
         out_shape=(
             jax.ShapeDtypeStruct((fin, dim), bf),
             jax.ShapeDtypeStruct((classes, dim), bf),
         ),
-        in_specs=[anywhere, anywhere, whole, whole],
+        in_specs=[anywhere] * 4,
         out_specs=(anywhere, whole),
         scratch_shapes=[
-            vmem((rows, fin), bf), vmem((fin, dim), bf), vmem((PLANE * rows, wide), bf),
+            vmem((PLANE, nz, wide, LANES), bf), vmem((rows, fin), bf), vmem((fin, dim), bf), vmem((classes, dim), bf),
+            vmem((1, rows), jnp.int32), vmem((PLANE * rows, wide), bf),
             vmem((rows, dim), bf), vmem((rows, dim), bf), vmem((PLANE * rows, dim), bf),
             vmem((classes, dim), bf), vmem((rows, LANES), f32), vmem((rows, LANES), f32),
             vmem((rows, classes), bf), vmem((PLANE * rows, classes // PLANE), bf),
             vmem((rows, dim), bf), vmem((rows, dim), bf), vmem((PLANE * rows, dim), bf),
             vmem((classes // PLANE, dim), f32), vmem((nz, classes // PLANE // nz, dim), f32),
-            vmem((classes, dim), bf), vmem((nz, wide, LANES), f32),
-            vmem((nz, wide, LANES), bf), vmem((nz, wide, LANES), bf), vmem((nz, wide, LANES), bf),
-            vmem((PLANE, nz, wide, LANES), bf),
+            vmem((nz, wide, LANES), f32), vmem((2, wide, LANES), bf), vmem((2, wide, LANES), bf),
+            vmem((wide, LANES), bf), vmem((wide, LANES), bf),
             dma((2 * steps,)), dma((3,)), dma((3,)), dma((4, PLANE - 1)), dma((4, PLANE - 1)),
-            dma((1,)), dma((nz - 1,)), dma((nz - 1,)), dma((nz - 1,)), dma((nz - 1,)),
-            dma((3,)), dma((3,)), dma((count, nz)), dma((count, nz)), dma((count, nz)),
-            dma((count, nz, 2)), dma((count, nz)), dma((count, nz)), dma((count, nz)),
-            dma((2, count, nz)), dma((2, count, nz)), dma((PLANE * nz,)),
+            dma((3,)), dma((nz - 1,)), dma((nz - 1,)), dma((nz - 1,)), dma((nz - 1,)),
+            dma((3,)), dma((3,)), dma((4, count)), dma((4, count)),
+            dma((2, count)), dma((2, count)), dma((4, count)), dma((4, count)),
+            dma((2, PLANE * nz)),
         ],
         compiler_params=pltpu.CompilerParams(
-            collective_id=0, has_side_effects=True, vmem_limit_bytes=52 * 2**20
+            collective_id=0, has_side_effects=True, vmem_limit_bytes=56 * 2**20
         ),
-    )(features, fc_weight, class_weight, labels.reshape(rows, 1))
+    )(features, fc_weight, class_weight, labels.reshape(1, rows))
+    return pl.pallas_call(
+        place,
+        out_shape=(
+            jax.ShapeDtypeStruct((fin, dim), bf),
+            jax.ShapeDtypeStruct((classes, dim), bf),
+        ),
+        in_specs=[anywhere, anywhere],
+        out_specs=(anywhere, anywhere),
+        scratch_shapes=[dma((steps + 1,))],
+        compiler_params=pltpu.CompilerParams(vmem_limit_bytes=56 * 2**20),
+    )(*results)
 
 
 def choose(n_dp, n_cls, features, fc_weight, class_weight, labels):
@@ -480,12 +476,11 @@
     fits = (
         n_cls == 2
         and n_dp % PLANE == 0
-        and nz > 1
+        and nz == 4
         and dim == nz * LANES
         and fin % LANES == 0
         and fin // LANES >= PLANE
-        and rows % 16 == 0
-        and rows <= 128
+        and rows == LANES
         and classes % (PLANE * LANES) == 0
         and classes // PLANE % (16 * nz) == 0
         and classes <= 512

time: 158 us -> 321 us (2.03)
  Pallas kernels: 148 us -> 320 us
  local copies, waits for them, and re-layouts: 8.57 us -> 0 us
    pallas_call x0 -> x1, Pallas kernels: none -> 212 us  [fused(): pl.pallas_call(place, out_shape=(jax.ShapeDtypeStruct((fin, dim), bf), ja...]
    pallas_call x1, Pallas kernels: 148 us -> 108 us  [fused(): pl.pallas_call(functools.partial(kernel, nz, chunks, rows * n_dp), out_sh...]
    unnamed x4 -> x0, local copies, waits for them, and re-layouts: 7.81 us -> none
where the time goes in v2:
time: 321 us
  Pallas kernels  320 us (100%)
    pallas_call x1, Pallas kernels, fused(): pl.pallas_call(place, out_shape=(jax.ShapeDtypeStruct((fin, dim), bf), ja...  212 us
    pallas_call x1, Pallas kernels, fused(): pl.pallas_call(functools.partial(kernel, nz, chunks, rows * n_dp), out_sh...  108 us

profile of v2, /device:TPU:1, one launch (start us, length us, event | category | flops | bytes accessed | tf_op | source)
XLA Modules:
  0.0 320.5 jit_solution(8812853108603875061)
XLA Ops:
  0.6 108.3 %shard_map.59 = (bf16[6272,512]{1,0:T(8,128)(2,1)}, bf16[512,512]{1,0:T(8,128)(2,1)}) custom-call(bf16[128,6272]{1,0:T(8,128)(2,1)} %feat_hbm.1, bf16[6272,512]{1,0:T(8,128)(2,1)} %w_hbm.1, bf16[512,512]{1,0:T(8,128)(2,1)} %cw_hbm.1, s32[1,128]{1,0:T(1,128)} %bitcast.1), custom_call_target="tpu_custom_call" | custom-call | tf_op jit(solution)/shard_map/pallas_call | solution.py:431
  108.9 211.6 %shard_map.60 = (bf16[6272,512]{1,0:T(8,128)(2,1)}, bf16[512,512]{1,0:T(8,128)(2,1)}) custom-call(bf16[6272,512]{1,0:T(8,128)(2,1)} %get-tuple-element.4.fc_in, bf16[512,512]{1,0:T(8,128)(2,1)} %get-tuple-element.5.class_in), custom_call_target="tpu_custom_call" | custom-call | tf_op jit(solution)/shard_map/pallas_call | solution.py:459

commit v3 on v2

--- a/solution.py
+++ b/solution.py
@@ -229,10 +229,10 @@
     is_target = columns == label
     powers, slopes = margin_terms(cosine, is_target)
     partial = jnp.sum(powers, axis=1, keepdims=True)
-    tot_s[...] = jnp.broadcast_to(partial, tot_s.shape)
+    tot_s[...] = jnp.broadcast_to(partial, (rows, LANES)).T[0:8, :]
     send(None, remote(lambda: tot_s, lambda: tot_r, lambda: x_send.at[1], lambda: x_recv.at[1], x_dev))
     landed(tot_r, x_recv.at[1])
-    totals = partial + tot_r[:, 0:1]
+    totals = partial + jnp.broadcast_to(tot_r[0:1, :], (LANES, rows)).T[:, 0:1]
     weight = 1.0 / math.sqrt(faces_total)
     grad = ((powers / totals - is_target.astype(jnp.float32)) * weight * slopes).astype(ROUNDED)
     cosg[...] = grad
@@ -403,17 +403,9 @@
         copy.wait()
 
 
-def place(fc_in, class_in, fc_out, class_out, sems):
-    pieces = sems.shape[0] - 1
-    size = fc_in.shape[0] // pieces
-    copies = [pltpu.make_async_copy(class_in, class_out, sems.at[pieces])]
-    for i in range(pieces):
-        part = pl.ds(i * size, size)
-        copies.append(pltpu.make_async_copy(fc_in.at[part, :], fc_out.at[part, :], sems.at[i]))
-    for copy in copies:
-        copy.start()
-    for copy in copies:
-        copy.wait()
+def place(fc_in, class_in, fc_out, class_out):
+    fc_out[...] = fc_in[...]
+    class_out[...] = class_in[...]
 
 
 def fused(n_dp, features, fc_weight, class_weight, labels):
@@ -422,7 +414,7 @@
     nz = n_dp // PLANE
     blocks = fin // LANES
     wide = (blocks - (PLANE - 1) * (blocks // PLANE)) * LANES
-    chunks = split_rows(wide // LANES, min(7, wide // LANES))
+    chunks = split_rows(wide // LANES, min(13, wide // LANES))
     count = len(chunks)
     steps = max(d for d in range(1, 9) if blocks % d == 0)
     bf, f32, dma = jnp.bfloat16, jnp.float32, pltpu.SemaphoreType.DMA
@@ -440,7 +432,7 @@
             vmem((PLANE, nz, wide, LANES), bf), vmem((rows, fin), bf), vmem((fin, dim), bf), vmem((classes, dim), bf),
             vmem((1, rows), jnp.int32), vmem((PLANE * rows, wide), bf),
             vmem((rows, dim), bf), vmem((rows, dim), bf), vmem((PLANE * rows, dim), bf),
-            vmem((classes, dim), bf), vmem((rows, LANES), f32), vmem((rows, LANES), f32),
+            vmem((classes, dim), bf), vmem((8, rows), f32), vmem((8, rows), f32),
             vmem((rows, classes), bf), vmem((PLANE * rows, classes // PLANE), bf),
             vmem((rows, dim), bf), vmem((rows, dim), bf), vmem((PLANE * rows, dim), bf),
             vmem((classes // PLANE, dim), f32), vmem((nz, classes // PLANE // nz, dim), f32),
@@ -456,15 +448,20 @@
             collective_id=0, has_side_effects=True, vmem_limit_bytes=56 * 2**20
         ),
     )(features, fc_weight, class_weight, labels.reshape(1, rows))
+    blocks_of = tuple(
+        pl.BlockSpec((size // steps if size % (16 * steps) == 0 else size, dim),
+                     (lambda i: (i, 0)) if size % (16 * steps) == 0 else (lambda i: (0, 0)))
+        for size in (fin, classes)
+    )
     return pl.pallas_call(
         place,
+        grid=(steps,),
         out_shape=(
             jax.ShapeDtypeStruct((fin, dim), bf),
             jax.ShapeDtypeStruct((classes, dim), bf),
         ),
-        in_specs=[anywhere, anywhere],
-        out_specs=(anywhere, anywhere),
-        scratch_shapes=[dma((steps + 1,))],
+        in_specs=blocks_of,
+        out_specs=blocks_of,
         compiler_params=pltpu.CompilerParams(vmem_limit_bytes=56 * 2**20),
     )(*results)
 

time: 321 us -> 119 us (0.37)
  Pallas kernels: 320 us -> 119 us
    pallas_call x1, Pallas kernels: 212 us -> 8.37 us  [fused(): pl.pallas_call(place, grid=(steps,), out_shape=(jax.ShapeDtypeStruct((fin...]
where the time goes in v3:
time: 119 us
  Pallas kernels  119 us (100%)
    pallas_call x1, Pallas kernels, fused(): pl.pallas_call(functools.partial(kernel, nz, chunks, rows * n_dp), out_sh...  110 us
    pallas_call x1, Pallas kernels, fused(): pl.pallas_call(place, grid=(steps,), out_shape=(jax.ShapeDtypeStruct((fin...  8.37 us

profile of v3, /device:TPU:1, one launch (start us, length us, event | category | flops | bytes accessed | tf_op | source)
XLA Modules:
  0.0 119.2 jit_solution(9863963273721103332)
XLA Ops:
  0.6 110.2 %shard_map.59 = (bf16[6272,512]{1,0:T(8,128)(2,1)}, bf16[512,512]{1,0:T(8,128)(2,1)}) custom-call(bf16[128,6272]{1,0:T(8,128)(2,1)} %feat_hbm.1, bf16[6272,512]{1,0:T(8,128)(2,1)} %w_hbm.1, bf16[512,512]{1,0:T(8,128)(2,1)} %cw_hbm.1, s32[1,128]{1,0:T(1,128)} %bitcast.1), custom_call_target="tpu_custom_call" | custom-call | tf_op jit(solution)/shard_map/pallas_call | solution.py:423
  110.8 8.4 %shard_map.60 = (bf16[6272,512]{1,0:T(8,128)(2,1)}, bf16[512,512]{1,0:T(8,128)(2,1)}) custom-call(bf16[6272,512]{1,0:T(8,128)(2,1)} %get-tuple-element.4.fc_in, bf16[512,512]{1,0:T(8,128)(2,1)} %get-tuple-element.5.class_in), custom_call_target="tpu_custom_call" | custom-call | tf_op jit(solution)/shard_map/pallas_call | solution.py:456

commit v4 on v3

--- a/solution.py
+++ b/solution.py
@@ -102,11 +102,21 @@
 def kernel(
     nz, chunks, faces_total,
     feat_hbm, w_hbm, cw_hbm, lab_hbm,
-    fc_out, cout,
-    slab, feat, w, cw_ref, lab_ref, gath, praw, rraw, unit_all, cu, tot_s, tot_r, cosg, cg_all, pgrad, rgrad,
+    *refs,
+):
+    count = len(chunks)
+    slabs, refs = refs[:count], refs[count:]
+    kernel_body(nz, chunks, faces_total, feat_hbm, w_hbm, cw_hbm, lab_hbm, slabs, *refs)
+
+
+def kernel_body(
+    nz, chunks, faces_total,
+    feat_hbm, w_hbm, cw_hbm, lab_hbm,
+    slabs, cout,
+    feat, w, cw_ref, lab_ref, gath, praw, rraw, unit_all, cu, tot_s, tot_r, cosg, cg_all, pgrad, rgrad,
     rg_all, cpart, cslots, f, send1, recv1, send2, recv2,
     load_sem, x_send, x_recv, p_send, p_recv, own_sem, c_send, c_recv,
-    ca_send, ca_recv, cp_send, cp_recv, z_send, z_recv, y_send, y_recv, n_send, n_recv, out_sem,
+    ca_send, ca_recv, cp_send, cp_recv, z_send, z_recv, y_send, y_recv, n_send, n_recv,
 ):
     rows, fin = feat.shape
     classes, dim = cw_ref.shape
@@ -188,13 +198,6 @@
         feat_hbm.at[:, pl.ds(pl.multiple_of(q * per, LANES), wide)], gath.at[mine, :], own_sem.at[0]
     )
     own_feat.start()
-    for i, p in enumerate(plane):
-        cols = pl.ds(pl.multiple_of(p * per, LANES), wide)
-        send(None, remote(
-            lambda cols=cols: feat_hbm.at[:, cols], lambda: gath.at[mine, :],
-            lambda i=i: p_send.at[0, i], lambda i=i: p_recv.at[0, i], {"dp": z * PLANE + p},
-        ))
-
     total = jnp.zeros((rows, dim), jnp.float32)
     for k in range(steps):
         for copy in loads[k]:
@@ -203,6 +206,13 @@
         total = total + jnp.dot(feat[:, part], w[part, :], preferred_element_type=jnp.float32)
     praw[...] = total.astype(ROUNDED)
     send(None, remote(lambda: praw, lambda: rraw, lambda: x_send.at[0], lambda: x_recv.at[0], x_dev))
+
+    for i, p in enumerate(plane):
+        cols = pl.ds(pl.multiple_of(p * per, LANES), wide)
+        send(None, remote(
+            lambda cols=cols: feat.at[:, cols], lambda: gath.at[mine, :],
+            lambda i=i: p_send.at[0, i], lambda i=i: p_recv.at[0, i], {"dp": z * PLANE + p},
+        ))
 
     for copy in small:
         copy.wait()
@@ -276,16 +286,14 @@
         landed(rg_all.at[theirs, :], p_recv.at[3, i])
 
     count = len(chunks)
-    split = max(count - 3, 0)
-    writes = []
 
     def exchange(src, dst, sends, recvs, dev, *spot):
         send(None, remote(
             lambda: src, lambda: dst, lambda: sends.at[spot], lambda: recvs.at[spot], dev,
         ))
 
-    def pair(p, which, part):
-        return slab.at[p, pl.ds(which * 2, 2), part, :]
+    def pair(c, p, which):
+        return slabs[c].at[p, pl.ds(which * 2, 2), :, :]
 
     def multiply(c, part):
         product = lax.dot_general(
@@ -306,50 +314,37 @@
 
     def sum_far(c, part):
         landed(recv2.at[part, :], z_recv.at[1, c])
-        slab[q, owned, part, :] = (
+        slabs[c][q, owned, :, :] = (
             f[owned, part, :]
             + recv1[half, part, :].astype(jnp.float32)
             + recv2[part, :].astype(jnp.float32)
         ).astype(ROUNDED)
-        block = slab.at[q, owned, part, :]
+        block = slabs[c].at[q, owned, :, :]
         exchange(block, block, z_send, z_recv, far, 2, c)
 
     def gather_far(c, part):
-        landed(slab.at[q, side * 2 + 1 - half, part, :], z_recv.at[2, c])
-        block = pair(q, side, part)
+        landed(slabs[c].at[q, side * 2 + 1 - half, :, :], z_recv.at[2, c])
+        block = pair(c, q, side)
         exchange(block, block, z_send, z_recv, near, 3, c)
         exchange(block, block, y_send, y_recv, y_dev, side, c)
         exchange(block, block, n_send, n_recv, c_dev, side, c)
 
     def gather_near(c, part):
-        block = pair(q, 1 - side, part)
+        block = pair(c, q, 1 - side)
         landed(block, z_recv.at[3, c])
         exchange(block, block, y_send, y_recv, y_dev, 1 - side, c)
         exchange(block, block, n_send, n_recv, c_dev, 1 - side, c)
 
     def gather_across(c, part):
         for which in (side, 1 - side):
-            block = pair(q_y, which, part)
+            block = pair(c, q_y, which)
             landed(block, y_recv.at[which, c])
             exchange(block, block, n_send, n_recv, c_dev, 2 + which, c)
 
     def gather_core(c, part):
         for which in range(2):
-            landed(pair(q_c, which, part), n_recv.at[which, c])
-            landed(pair(q_d, which, part), n_recv.at[2 + which, c])
-        if c in (split, count - 1):
-            low = 0 if c == split else chunks[split + 1][0]
-            high = part.start + part.size
-            for p in range(PLANE):
-                size = (high if p == PLANE - 1 else min(high, per)) - low
-                for j in range(nz):
-                    copy = pltpu.make_async_copy(
-                        slab.at[p, j, pl.ds(low, size), :],
-                        fc_out.at[pl.ds(p * per + low, size), pl.ds(j * LANES, LANES)],
-                        out_sem.at[int(c != split), p * nz + j],
-                    )
-                    copy.start()
-                    writes.append(copy)
+            landed(pair(c, q_c, which), n_recv.at[which, c])
+            landed(pair(c, q_d, which), n_recv.at[2 + which, c])
 
     def class_rows():
         for i, t in enumerate(line_from):
@@ -399,13 +394,27 @@
     landed(cout.at[at(q_d, cq), :], cp_recv.at[2])
     for cond, make in pending:
         make().wait_send()
-    for copy in writes:
+
+
+def place(chunks, per, *refs):
+    count = len(chunks)
+    slabs, cout = refs[:count], refs[count]
+    fc_out, class_out, rows_of, sems = refs[count + 1:]
+    copies = [pltpu.make_async_copy(cout, class_out, sems.at[0])]
+    copies[0].start()
+    for p in range(PLANE):
+        for c, (first, size) in enumerate(chunks):
+            size = size if p == PLANE - 1 else min(size, per - first)
+            if size > 0:
+                start = p * per + first
+                for j in range(slabs[c].shape[1]):
+                    rows_of[pl.ds(start, size), pl.ds(j * LANES, LANES)] = slabs[c][p, j, pl.ds(0, size), :]
+                copies.append(pltpu.make_async_copy(
+                    rows_of.at[pl.ds(start, size), :], fc_out.at[pl.ds(start, size), :], sems.at[len(copies)],
+                ))
+                copies[-1].start()
+    for copy in copies:
         copy.wait()
-
-
-def place(fc_in, class_in, fc_out, class_out):
-    fc_out[...] = fc_in[...]
-    class_out[...] = class_in[...]
 
 
 def fused(n_dp, features, fc_weight, class_weight, labels):
@@ -414,7 +423,7 @@
     nz = n_dp // PLANE
     blocks = fin // LANES
     wide = (blocks - (PLANE - 1) * (blocks // PLANE)) * LANES
-    chunks = split_rows(wide // LANES, min(13, wide // LANES))
+    chunks = split_rows(wide // LANES, min(7, wide // LANES))
     count = len(chunks)
     steps = max(d for d in range(1, 9) if blocks % d == 0)
     bf, f32, dma = jnp.bfloat16, jnp.float32, pltpu.SemaphoreType.DMA
@@ -423,13 +432,13 @@
     results = pl.pallas_call(
         functools.partial(kernel, nz, chunks, rows * n_dp),
         out_shape=(
-            jax.ShapeDtypeStruct((fin, dim), bf),
+            *[jax.ShapeDtypeStruct((PLANE, nz, size, LANES), bf) for _, size in chunks],
             jax.ShapeDtypeStruct((classes, dim), bf),
         ),
         in_specs=[anywhere] * 4,
-        out_specs=(anywhere, whole),
+        out_specs=(whole,) * (count + 1),
         scratch_shapes=[
-            vmem((PLANE, nz, wide, LANES), bf), vmem((rows, fin), bf), vmem((fin, dim), bf), vmem((classes, dim), bf),
+            vmem((rows, fin), bf), vmem((fin, dim), bf), vmem((classes, dim), bf),
             vmem((1, rows), jnp.int32), vmem((PLANE * rows, wide), bf),
             vmem((rows, dim), bf), vmem((rows, dim), bf), vmem((PLANE * rows, dim), bf),
             vmem((classes, dim), bf), vmem((8, rows), f32), vmem((8, rows), f32),
@@ -442,27 +451,21 @@
             dma((3,)), dma((nz - 1,)), dma((nz - 1,)), dma((nz - 1,)), dma((nz - 1,)),
             dma((3,)), dma((3,)), dma((4, count)), dma((4, count)),
             dma((2, count)), dma((2, count)), dma((4, count)), dma((4, count)),
-            dma((2, PLANE * nz)),
         ],
         compiler_params=pltpu.CompilerParams(
-            collective_id=0, has_side_effects=True, vmem_limit_bytes=56 * 2**20
+            collective_id=0, has_side_effects=True, vmem_limit_bytes=46 * 2**20
         ),
     )(features, fc_weight, class_weight, labels.reshape(1, rows))
-    blocks_of = tuple(
-        pl.BlockSpec((size // steps if size % (16 * steps) == 0 else size, dim),
-                     (lambda i: (i, 0)) if size % (16 * steps) == 0 else (lambda i: (0, 0)))
-        for size in (fin, classes)
-    )
     return pl.pallas_call(
-        place,
-        grid=(steps,),
+        functools.partial(place, chunks, blocks // PLANE * LANES),
         out_shape=(
             jax.ShapeDtypeStruct((fin, dim), bf),
             jax.ShapeDtypeStruct((classes, dim), bf),
         ),
-        in_specs=blocks_of,
-        out_specs=blocks_of,
-        compiler_params=pltpu.CompilerParams(vmem_limit_bytes=56 * 2**20),
+        in_specs=[whole] * (count + 1),
+        out_specs=(anywhere, anywhere),
+        scratch_shapes=[vmem((fin, dim), bf), dma((PLANE * count + 1,))],
+        compiler_params=pltpu.CompilerParams(vmem_limit_bytes=16 * 2**20),
     )(*results)
 
 

time: 119 us -> 114 us (0.958)
  Pallas kernels: 119 us -> 111 us
  local copies, waits for them, and re-layouts: 0 us -> 1.69 us
    pallas_call x1, Pallas kernels: 8.37 us -> 3.07 us  [fused(): pl.pallas_call(functools.partial(place, chunks, blocks // PLANE * LANES),...]
    pallas_call x1, Pallas kernels: 110 us -> 108 us  [fused(): pl.pallas_call(functools.partial(kernel, nz, chunks, rows * n_dp), out_sh...]
    unnamed x0 -> x4, local copies, waits for them, and re-layouts: none -> 1.69 us
where the time goes in v4:
time: 114 us
  Pallas kernels  111 us (97%)
  local copies, waits for them, and re-layouts  1.69 us (1%)
    pallas_call x1, Pallas kernels, fused(): pl.pallas_call(functools.partial(kernel, nz, chunks, rows * n_dp), out_sh...  108 us
    pallas_call x1, Pallas kernels, fused(): pl.pallas_call(functools.partial(place, chunks, blocks // PLANE * LANES),...  3.07 us

profile of v4, /device:TPU:1, one launch (start us, length us, event | category | flops | bytes accessed | tf_op | source)
XLA Modules:
  0.0 113.8 jit_solution(13892475391849208823)
XLA Ops:
  0.6 0.0 copy-start
  0.6 1.0 copy-done
  1.7 0.0 copy-start.1
  1.7 0.7 copy-done.1
  2.3 108.4 %shard_map.59 = (bf16[4,4,256,128]{3,2,1,0:T(8,128)(2,1)S(1)}, bf16[4,4,256,128]{3,2,1,0:T(8,128)(2,1)S(1)}, bf16[4,4,256,128]{3,2,1,0:T(8,128)(2,1)S(1)}, bf16[...) custom-call(bf16[128,6272]{1,0:T(8,128)(2,1)} %feat_hbm.1, ...), custom_call_target="tpu_custom_call" | custom-call | tf_op jit(solution)/shard_map/pallas_call | solution.py:432
  110.7 3.1 %shard_map.60 = (bf16[6272,512]{1,0:T(8,128)(2,1)}, bf16[512,512]{1,0:T(8,128)(2,1)}) custom-call(bf16[4,4,256,128]{3,2,1,0:T(8,128)(2,1)S(1)} %get-tuple-element.10.refs_0_, bf16[4,4,256,128]{3,2,1,0:T(8,128)(2,1)S(1)} %get-tuple-element.11.refs_1_, bf16[4,4,256,128]{3,2,1,0:T(8,128)(2,1)S(1)} %get-tuple-element.12.refs_2_, ...), custom_call_target="tpu_custom_call" | custom-call | tf_op jit(solution)/shard_map/pallas_call | solution.py:459
Async XLA Ops:
  0.6 1.0 copy-start
  1.7 0.7 copy-start.1

commit v5 on v4

--- a/solution.py
+++ b/solution.py
@@ -89,14 +89,10 @@
 ROUNDED = jnp.bfloat16
 
 
-def split_rows(blocks, parts):
-    base, more = divmod(blocks, parts)
-    runs, start = [], 0
-    for part in range(parts):
-        size = base + (1 if part < more else 0)
-        runs.append((start * LANES, size * LANES))
-        start += size
-    return runs
+def split_rows(blocks):
+    sizes = [1] + [2] * ((blocks - 1) // 2)
+    sizes += [1] * (blocks - sum(sizes))
+    return [(sum(sizes[:i]) * LANES, size * LANES) for i, size in enumerate(sizes)]
 
 
 def kernel(
@@ -174,18 +170,16 @@
     ]
     for copy in small:
         copy.start()
-    steps = load_sem.shape[0] // 2
+    steps = load_sem.shape[0]
     kk = fin // steps
+    feat_load = pltpu.make_async_copy(feat_hbm, feat, own_sem.at[3])
+    feat_load.start()
     loads = []
     for k in range(steps):
         part = pl.ds(k * kk, kk)
-        pair = (
-            pltpu.make_async_copy(w_hbm.at[part, :], w.at[part, :], load_sem.at[2 * k]),
-            pltpu.make_async_copy(feat_hbm.at[:, part], feat.at[:, part], load_sem.at[2 * k + 1]),
-        )
-        for copy in pair:
-            copy.start()
-        loads.append(pair)
+        copy = pltpu.make_async_copy(w_hbm.at[part, :], w.at[part, :], load_sem.at[k])
+        copy.start()
+        loads.append(copy)
 
     barrier = pltpu.get_barrier_semaphore()
     peers = [x_dev] + [{"dp": z * PLANE + p} for p in plane] + [{"dp": t * PLANE + q} for t in line]
@@ -198,15 +192,7 @@
         feat_hbm.at[:, pl.ds(pl.multiple_of(q * per, LANES), wide)], gath.at[mine, :], own_sem.at[0]
     )
     own_feat.start()
-    total = jnp.zeros((rows, dim), jnp.float32)
-    for k in range(steps):
-        for copy in loads[k]:
-            copy.wait()
-        part = pl.ds(k * kk, kk)
-        total = total + jnp.dot(feat[:, part], w[part, :], preferred_element_type=jnp.float32)
-    praw[...] = total.astype(ROUNDED)
-    send(None, remote(lambda: praw, lambda: rraw, lambda: x_send.at[0], lambda: x_recv.at[0], x_dev))
-
+    feat_load.wait()
     for i, p in enumerate(plane):
         cols = pl.ds(pl.multiple_of(p * per, LANES), wide)
         send(None, remote(
@@ -214,6 +200,14 @@
             lambda i=i: p_send.at[0, i], lambda i=i: p_recv.at[0, i], {"dp": z * PLANE + p},
         ))
 
+    total = jnp.zeros((rows, dim), jnp.float32)
+    for k in range(steps):
+        loads[k].wait()
+        part = pl.ds(k * kk, kk)
+        total = total + jnp.dot(feat[:, part], w[part, :], preferred_element_type=jnp.float32)
+    praw[...] = total.astype(ROUNDED)
+    send(None, remote(lambda: praw, lambda: rraw, lambda: x_send.at[0], lambda: x_recv.at[0], x_dev))
+
     for copy in small:
         copy.wait()
     class_f = cw_ref[...].astype(jnp.float32)
@@ -226,10 +220,10 @@
     unit_f = raw / norm
     unit = unit_f.astype(ROUNDED)
     unit_all[mine, :] = unit
-    for i, p in enumerate(plane):
+    for i, dev in enumerate((y_dev, c_dev)):
         send(None, remote(
             lambda: unit_all.at[mine, :], lambda: unit_all.at[mine, :],
-            lambda i=i: p_send.at[1, i], lambda i=i: p_recv.at[1, i], {"dp": z * PLANE + p},
+            lambda i=i: p_send.at[1, i], lambda i=i: p_recv.at[1, i], dev,
         ))
     cosine = lax.dot_general(
         unit, cu[...], (((1,), (1,)), ((), ())), preferred_element_type=jnp.float32
@@ -266,10 +260,16 @@
             lambda i=i: p_send.at[3, i], lambda i=i: p_recv.at[3, i], {"dp": z * PLANE + p},
         ))
 
+    across = at(q_y, rows)
+    landed(unit_all.at[across, :], p_recv.at[1, 0])
+    send(None, remote(
+        lambda: unit_all.at[across, :], lambda: unit_all.at[across, :],
+        lambda: p_send.at[1, 2], lambda: p_recv.at[1, 2], c_dev,
+    ))
     for i, p in enumerate(plane_from):
-        theirs = at(p, rows)
-        landed(unit_all.at[theirs, :], p_recv.at[1, i])
-        landed(cg_all.at[theirs, :], p_recv.at[2, i])
+        landed(cg_all.at[at(p, rows), :], p_recv.at[2, i])
+    landed(unit_all.at[at(q_c, rows), :], p_recv.at[1, 1])
+    landed(unit_all.at[at(q_d, rows), :], p_recv.at[1, 2])
     cpart[...] = lax.dot_general(
         cg_all[...], unit_all[...], (((0,), (0,)), ((), ())), preferred_element_type=jnp.float32
     )
@@ -287,64 +287,84 @@
 
     count = len(chunks)
 
-    def exchange(src, dst, sends, recvs, dev, *spot):
-        send(None, remote(
-            lambda: src, lambda: dst, lambda: sends.at[spot], lambda: recvs.at[spot], dev,
+    def has(c, owner):
+        return owner == PLANE - 1 if chunks[c][0] >= per else None
+
+    def only(cond, body):
+        if cond is None:
+            body()
+        else:
+            pl.when(cond)(body)
+
+    def exchange(cond, src, dst, sends, recvs, dev, *spot):
+        send(cond, remote(
+            lambda: src(), lambda: dst(), lambda: sends.at[spot], lambda: recvs.at[spot], dev,
         ))
 
     def pair(c, p, which):
         return slabs[c].at[p, pl.ds(which * 2, 2), :, :]
 
     def multiply(c, part):
-        product = lax.dot_general(
-            gath[:, part], rg_all[...], (((0,), (0,)), ((), ())), preferred_element_type=jnp.float32
+        def body():
+            product = lax.dot_general(
+                gath[:, part], rg_all[...], (((0,), (0,)), ((), ())), preferred_element_type=jnp.float32
+            )
+            for j in range(nz):
+                f[j, part, :] = product[:, j * LANES:(j + 1) * LANES]
+            for i in range(2):
+                send1[i, part, :] = f[(1 - side) * 2 + i, part, :].astype(ROUNDED)
+
+        only(has(c, q), body)
+        exchange(
+            has(c, q), lambda: send1.at[:, part, :], lambda: recv1.at[:, part, :], z_send, z_recv, near, 0, c
         )
-        for j in range(nz):
-            f[j, part, :] = product[:, j * LANES:(j + 1) * LANES]
-        for i in range(2):
-            send1[i, part, :] = f[(1 - side) * 2 + i, part, :].astype(ROUNDED)
-        exchange(send1.at[:, part, :], recv1.at[:, part, :], z_send, z_recv, near, 0, c)
 
     def sum_near(c, part):
-        landed(recv1.at[:, part, :], z_recv.at[0, c])
-        send2[part, :] = (
-            f[side * 2 + 1 - half, part, :] + recv1[1 - half, part, :].astype(jnp.float32)
-        ).astype(ROUNDED)
-        exchange(send2.at[part, :], recv2.at[part, :], z_send, z_recv, far, 1, c)
+        def body():
+            landed(recv1.at[:, part, :], z_recv.at[0, c])
+            send2[part, :] = (
+                f[side * 2 + 1 - half, part, :] + recv1[1 - half, part, :].astype(jnp.float32)
+            ).astype(ROUNDED)
+
+        only(has(c, q), body)
+        exchange(has(c, q), lambda: send2.at[part, :], lambda: recv2.at[part, :], z_send, z_recv, far, 1, c)
 
     def sum_far(c, part):
-        landed(recv2.at[part, :], z_recv.at[1, c])
-        slabs[c][q, owned, :, :] = (
-            f[owned, part, :]
-            + recv1[half, part, :].astype(jnp.float32)
-            + recv2[part, :].astype(jnp.float32)
-        ).astype(ROUNDED)
-        block = slabs[c].at[q, owned, :, :]
-        exchange(block, block, z_send, z_recv, far, 2, c)
+        def body():
+            landed(recv2.at[part, :], z_recv.at[1, c])
+            slabs[c][q, owned, :, :] = (
+                f[owned, part, :]
+                + recv1[half, part, :].astype(jnp.float32)
+                + recv2[part, :].astype(jnp.float32)
+            ).astype(ROUNDED)
+
+        only(has(c, q), body)
+        block = lambda: slabs[c].at[q, owned, :, :]
+        exchange(has(c, q), block, block, z_send, z_recv, far, 2, c)
 
     def gather_far(c, part):
-        landed(slabs[c].at[q, side * 2 + 1 - half, :, :], z_recv.at[2, c])
-        block = pair(c, q, side)
-        exchange(block, block, z_send, z_recv, near, 3, c)
-        exchange(block, block, y_send, y_recv, y_dev, side, c)
-        exchange(block, block, n_send, n_recv, c_dev, side, c)
+        only(has(c, q), lambda: landed(slabs[c].at[q, side * 2 + 1 - half, :, :], z_recv.at[2, c]))
+        block = lambda: pair(c, q, side)
+        exchange(has(c, q), block, block, z_send, z_recv, near, 3, c)
+        exchange(has(c, q), block, block, y_send, y_recv, y_dev, side, c)
+        exchange(has(c, q), block, block, n_send, n_recv, c_dev, side, c)
 
     def gather_near(c, part):
-        block = pair(c, q, 1 - side)
-        landed(block, z_recv.at[3, c])
-        exchange(block, block, y_send, y_recv, y_dev, 1 - side, c)
-        exchange(block, block, n_send, n_recv, c_dev, 1 - side, c)
+        block = lambda: pair(c, q, 1 - side)
+        only(has(c, q), lambda: landed(block(), z_recv.at[3, c]))
+        exchange(has(c, q), block, block, y_send, y_recv, y_dev, 1 - side, c)
+        exchange(has(c, q), block, block, n_send, n_recv, c_dev, 1 - side, c)
 
     def gather_across(c, part):
         for which in (side, 1 - side):
-            block = pair(c, q_y, which)
-            landed(block, y_recv.at[which, c])
-            exchange(block, block, n_send, n_recv, c_dev, 2 + which, c)
+            block = lambda which=which: pair(c, q_y, which)
+            only(has(c, q_y), lambda: landed(block(), y_recv.at[which, c]))
+            exchange(has(c, q_y), block, block, n_send, n_recv, c_dev, 2 + which, c)
 
     def gather_core(c, part):
         for which in range(2):
-            landed(pair(c, q_c, which), n_recv.at[which, c])
-            landed(pair(c, q_d, which), n_recv.at[2 + which, c])
+            only(has(c, q_c), lambda: landed(pair(c, q_c, which), n_recv.at[which, c]))
+            only(has(c, q_d), lambda: landed(pair(c, q_d, which), n_recv.at[2 + which, c]))
 
     def class_rows():
         for i, t in enumerate(line_from):
@@ -377,10 +397,13 @@
         block = lambda: cout.at[at(q_y, cq), :]
         send(None, remote(block, block, lambda: cp_send.at[2], lambda: cp_recv.at[2], c_dev))
 
-    stages = (multiply, sum_near, sum_far, gather_far, gather_near, gather_across, gather_core)
-    for tick in range(count + len(stages) - 1):
-        for stage, run in enumerate(stages):
-            c = tick - stage
+    stages = (
+        (0, multiply), (1, sum_near), (2, sum_far), (3, gather_far), (4, gather_near),
+        (6, gather_across), (8, gather_core),
+    )
+    for tick in range(count + stages[-1][0]):
+        for late, run in stages:
+            c = tick - late
             if 0 <= c < count:
                 run(c, pl.ds(*chunks[c]))
         if tick == 1:
@@ -393,7 +416,7 @@
     landed(cout.at[at(q_c, cq), :], cp_recv.at[1])
     landed(cout.at[at(q_d, cq), :], cp_recv.at[2])
     for cond, make in pending:
-        make().wait_send()
+        only(cond, lambda: make().wait_send())
 
 
 def place(chunks, per, *refs):
@@ -404,8 +427,7 @@
     copies[0].start()
     for p in range(PLANE):
         for c, (first, size) in enumerate(chunks):
-            size = size if p == PLANE - 1 else min(size, per - first)
-            if size > 0:
+            if p == PLANE - 1 or first < per:
                 start = p * per + first
                 for j in range(slabs[c].shape[1]):
                     rows_of[pl.ds(start, size), pl.ds(j * LANES, LANES)] = slabs[c][p, j, pl.ds(0, size), :]
@@ -423,7 +445,10 @@
     nz = n_dp // PLANE
     blocks = fin // LANES
     wide = (blocks - (PLANE - 1) * (blocks // PLANE)) * LANES
-    chunks = split_rows(wide // LANES, min(7, wide // LANES))
+    per = blocks // PLANE
+    chunks = split_rows(per)
+    if wide // LANES > per:
+        chunks.append((per * LANES, wide - per * LANES))
     count = len(chunks)
     steps = max(d for d in range(1, 9) if blocks % d == 0)
     bf, f32, dma = jnp.bfloat16, jnp.float32, pltpu.SemaphoreType.DMA
@@ -447,8 +472,8 @@
             vmem((classes // PLANE, dim), f32), vmem((nz, classes // PLANE // nz, dim), f32),
             vmem((nz, wide, LANES), f32), vmem((2, wide, LANES), bf), vmem((2, wide, LANES), bf),
             vmem((wide, LANES), bf), vmem((wide, LANES), bf),
-            dma((2 * steps,)), dma((3,)), dma((3,)), dma((4, PLANE - 1)), dma((4, PLANE - 1)),
-            dma((3,)), dma((nz - 1,)), dma((nz - 1,)), dma((nz - 1,)), dma((nz - 1,)),
+            dma((steps,)), dma((3,)), dma((3,)), dma((4, PLANE - 1)), dma((4, PLANE - 1)),
+            dma((4,)), dma((nz - 1,)), dma((nz - 1,)), dma((nz - 1,)), dma((nz - 1,)),
             dma((3,)), dma((3,)), dma((4, count)), dma((4, count)),
             dma((2, count)), dma((2, count)), dma((4, count)), dma((4, count)),
         ],

time: 114 us -> 107 us (0.939)
  Pallas kernels: 111 us -> 104 us
    pallas_call x1, Pallas kernels: 108 us -> 101 us  [fused(): pl.pallas_call(functools.partial(kernel, nz, chunks, rows * n_dp), out_sh...]
where the time goes in v5:
time: 107 us; the launch traced here: 106 us
  Pallas kernels  104 us (97%)
  local copies, waits for them, and re-layouts  1.69 us (2%)
    pallas_call x1, Pallas kernels, fused(): pl.pallas_call(functools.partial(kernel, nz, chunks, rows * n_dp), out_sh...  101 us
    pallas_call x1, Pallas kernels, fused(): pl.pallas_call(functools.partial(place, chunks, blocks // PLANE * LANES),...  3.11 us

profile of v5, /device:TPU:1, one launch (start us, length us, event | category | flops | bytes accessed | tf_op | source)
XLA Modules:
  0.0 106.3 jit_solution(10997029579464603600)
XLA Ops:
  0.6 0.0 copy-start
  0.6 1.0 copy-done
  1.7 0.0 copy-start.1
  1.7 0.7 copy-done.1
  2.3 100.8 %shard_map.59 = (bf16[4,4,128,128]{3,2,1,0:T(8,128)(2,1)S(1)}, bf16[4,4,256,128]{3,2,1,0:T(8,128)(2,1)S(1)}, bf16[4,4,256,128]{3,2,1,0:T(8,128)(2,1)S(1)}, bf16[...) custom-call(bf16[128,6272]{1,0:T(8,128)(2,1)} %feat_hbm.1, ...), custom_call_target="tpu_custom_call" | custom-call | tf_op jit(solution)/shard_map/pallas_call | solution.py:457
  103.2 3.1 %shard_map.60 = (bf16[6272,512]{1,0:T(8,128)(2,1)}, bf16[512,512]{1,0:T(8,128)(2,1)}) custom-call(bf16[4,4,128,128]{3,2,1,0:T(8,128)(2,1)S(1)} %get-tuple-element.11.refs_0_, bf16[4,4,256,128]{3,2,1,0:T(8,128)(2,1)S(1)} %get-tuple-element.12.refs_1_, bf16[4,4,256,128]{3,2,1,0:T(8,128)(2,1)S(1)} %get-tuple-element.13.refs_2_, ...), custom_call_target="tpu_custom_call" | custom-call | tf_op jit(solution)/shard_map/pallas_call | solution.py:484
Async XLA Ops:
  0.6 1.0 copy-start
  1.7 0.7 copy-start.1

commit v6 on v5

--- a/solution.py
+++ b/solution.py
@@ -134,6 +134,7 @@
     near = {"dp": (half * 2 + 1 - side) * PLANE + q}
     far = {"dp": ((1 - half) * 2 + side) * PLANE + q}
     owned = side * 2 + half
+    beside = side * 2 + 1 - half
     plane = [(q + d) % PLANE for d in range(1, PLANE)]
     plane_from = [(q + PLANE - d) % PLANE for d in range(1, PLANE)]
     line = [(z + d) % nz for d in range(1, nz)]
@@ -200,13 +201,21 @@
             lambda i=i: p_send.at[0, i], lambda i=i: p_recv.at[0, i], {"dp": z * PLANE + p},
         ))
 
-    total = jnp.zeros((rows, dim), jnp.float32)
-    for k in range(steps):
-        loads[k].wait()
-        part = pl.ds(k * kk, kk)
-        total = total + jnp.dot(feat[:, part], w[part, :], preferred_element_type=jnp.float32)
-    praw[...] = total.astype(ROUNDED)
-    send(None, remote(lambda: praw, lambda: rraw, lambda: x_send.at[0], lambda: x_recv.at[0], x_dev))
+    for h in range(2):
+        columns = pl.ds(h * (dim // 2), dim // 2)
+        total = jnp.zeros((rows, dim // 2), jnp.float32)
+        for k in range(steps):
+            if h == 0:
+                loads[k].wait()
+            part = pl.ds(k * kk, kk)
+            total = total + jnp.dot(
+                feat[:, part], w[part, columns], preferred_element_type=jnp.float32
+            )
+        praw[:, columns] = total.astype(ROUNDED)
+        send(None, remote(
+            lambda columns=columns: praw.at[:, columns], lambda columns=columns: rraw.at[:, columns],
+            lambda h=h: x_send.at[3 * h], lambda h=h: x_recv.at[3 * h], x_dev,
+        ))
 
     for copy in small:
         copy.wait()
@@ -214,7 +223,8 @@
     class_norm = jnp.sqrt(jnp.sum(class_f * class_f, axis=1, keepdims=True) + EPSILON)
     cu[...] = (class_f / class_norm).astype(ROUNDED)
 
-    landed(rraw, x_recv.at[0])
+    landed(rraw.at[:, pl.ds(0, dim // 2)], x_recv.at[0])
+    landed(rraw.at[:, pl.ds(dim // 2, dim // 2)], x_recv.at[3])
     raw = praw[...].astype(jnp.float32) + rraw[...].astype(jnp.float32)
     norm = jnp.sqrt(jnp.sum(raw * raw, axis=1, keepdims=True) + EPSILON)
     unit_f = raw / norm
@@ -341,30 +351,47 @@
         only(has(c, q), body)
         block = lambda: slabs[c].at[q, owned, :, :]
         exchange(has(c, q), block, block, z_send, z_recv, far, 2, c)
+        exchange(has(c, q), block, block, y_send, y_recv, y_dev, 0, c)
+        exchange(has(c, q), block, block, n_send, n_recv, c_dev, 0, c)
 
     def gather_far(c, part):
-        only(has(c, q), lambda: landed(slabs[c].at[q, side * 2 + 1 - half, :, :], z_recv.at[2, c]))
+        other = lambda: slabs[c].at[q, beside, :, :]
+        only(has(c, q), lambda: landed(other(), z_recv.at[2, c]))
         block = lambda: pair(c, q, side)
         exchange(has(c, q), block, block, z_send, z_recv, near, 3, c)
-        exchange(has(c, q), block, block, y_send, y_recv, y_dev, side, c)
-        exchange(has(c, q), block, block, n_send, n_recv, c_dev, side, c)
+        exchange(has(c, q), other, other, y_send, y_recv, y_dev, 1, c)
+        exchange(has(c, q), other, other, n_send, n_recv, c_dev, 1, c)
 
     def gather_near(c, part):
         block = lambda: pair(c, q, 1 - side)
         only(has(c, q), lambda: landed(block(), z_recv.at[3, c]))
-        exchange(has(c, q), block, block, y_send, y_recv, y_dev, 1 - side, c)
-        exchange(has(c, q), block, block, n_send, n_recv, c_dev, 1 - side, c)
+        exchange(has(c, q), block, block, y_send, y_recv, y_dev, 2, c)
+        exchange(has(c, q), block, block, n_send, n_recv, c_dev, 2, c)
+
+    def arrived(c, p, recvs, first):
+        landed(slabs[c].at[p, owned, :, :], recvs.at[first, c])
+        landed(slabs[c].at[p, beside, :, :], recvs.at[first + 1, c])
 
     def gather_across(c, part):
-        for which in (side, 1 - side):
+        for i, which in enumerate((side, 1 - side)):
             block = lambda which=which: pair(c, q_y, which)
-            only(has(c, q_y), lambda: landed(block(), y_recv.at[which, c]))
-            exchange(has(c, q_y), block, block, n_send, n_recv, c_dev, 2 + which, c)
+            if i == 0:
+                only(has(c, q_y), lambda: arrived(c, q_y, y_recv, 0))
+            else:
+                only(has(c, q_y), lambda: landed(block(), y_recv.at[2, c]))
+            exchange(has(c, q_y), block, block, n_send, n_recv, c_dev, 3 + i, c)
 
     def gather_core(c, part):
-        for which in range(2):
-            only(has(c, q_c), lambda: landed(pair(c, q_c, which), n_recv.at[which, c]))
-            only(has(c, q_d), lambda: landed(pair(c, q_d, which), n_recv.at[2 + which, c]))
+        def own():
+            arrived(c, q_c, n_recv, 0)
+            landed(pair(c, q_c, 1 - side), n_recv.at[2, c])
+
+        def crossed():
+            landed(pair(c, q_d, side), n_recv.at[3, c])
+            landed(pair(c, q_d, 1 - side), n_recv.at[4, c])
+
+        only(has(c, q_c), own)
+        only(has(c, q_d), crossed)
 
     def class_rows():
         for i, t in enumerate(line_from):
@@ -399,18 +426,18 @@
 
     stages = (
         (0, multiply), (1, sum_near), (2, sum_far), (3, gather_far), (4, gather_near),
-        (6, gather_across), (8, gather_core),
+        (7, gather_across), (9, gather_core),
     )
     for tick in range(count + stages[-1][0]):
         for late, run in stages:
             c = tick - late
             if 0 <= c < count:
                 run(c, pl.ds(*chunks[c]))
-        if tick == 1:
+        if tick == 3:
             class_rows()
-        if tick == 2:
+        if tick == 6:
             class_plane()
-        if tick == 3:
+        if tick == 9:
             class_across()
 
     landed(cout.at[at(q_c, cq), :], cp_recv.at[1])
@@ -472,10 +499,10 @@
             vmem((classes // PLANE, dim), f32), vmem((nz, classes // PLANE // nz, dim), f32),
             vmem((nz, wide, LANES), f32), vmem((2, wide, LANES), bf), vmem((2, wide, LANES), bf),
             vmem((wide, LANES), bf), vmem((wide, LANES), bf),
-            dma((steps,)), dma((3,)), dma((3,)), dma((4, PLANE - 1)), dma((4, PLANE - 1)),
+            dma((steps,)), dma((4,)), dma((4,)), dma((4, PLANE - 1)), dma((4, PLANE - 1)),
             dma((4,)), dma((nz - 1,)), dma((nz - 1,)), dma((nz - 1,)), dma((nz - 1,)),
             dma((3,)), dma((3,)), dma((4, count)), dma((4, count)),
-            dma((2, count)), dma((2, count)), dma((4, count)), dma((4, count)),
+            dma((3, count)), dma((3, count)), dma((5, count)), dma((5, count)),
         ],
         compiler_params=pltpu.CompilerParams(
             collective_id=0, has_side_effects=True, vmem_limit_bytes=46 * 2**20

time: 107 us -> 107 us (level)
  no operation moved by 1% of the time
where the time goes in v6:
time: 107 us; the launch traced here: 106 us
  Pallas kernels  104 us (97%)
  local copies, waits for them, and re-layouts  1.69 us (2%)
    pallas_call x1, Pallas kernels, fused(): pl.pallas_call(functools.partial(kernel, nz, chunks, rows * n_dp), out_sh...  101 us
    pallas_call x1, Pallas kernels, fused(): pl.pallas_call(functools.partial(place, chunks, blocks // PLANE * LANES),...  3.11 us

profile of v6, /device:TPU:1, one launch (start us, length us, event | category | flops | bytes accessed | tf_op | source)
XLA Modules:
  0.0 106.5 jit_solution(17755249975763661354)
XLA Ops:
  0.6 0.0 copy-start
  0.6 1.0 copy-done
  1.7 0.0 copy-start.1
  1.7 0.7 copy-done.1
  2.3 101.0 %shard_map.59 = (bf16[4,4,128,128]{3,2,1,0:T(8,128)(2,1)S(1)}, bf16[4,4,256,128]{3,2,1,0:T(8,128)(2,1)S(1)}, bf16[4,4,256,128]{3,2,1,0:T(8,128)(2,1)S(1)}, bf16[...) custom-call(bf16[128,6272]{1,0:T(8,128)(2,1)} %feat_hbm.1, ...), custom_call_target="tpu_custom_call" | custom-call | tf_op jit(solution)/shard_map/pallas_call | solution.py:484
  103.4 3.1 %shard_map.60 = (bf16[6272,512]{1,0:T(8,128)(2,1)}, bf16[512,512]{1,0:T(8,128)(2,1)}) custom-call(bf16[4,4,128,128]{3,2,1,0:T(8,128)(2,1)S(1)} %get-tuple-element.11.refs_0_, bf16[4,4,256,128]{3,2,1,0:T(8,128)(2,1)S(1)} %get-tuple-element.12.refs_1_, bf16[4,4,256,128]{3,2,1,0:T(8,128)(2,1)S(1)} %get-tuple-element.13.refs_2_, ...), custom_call_target="tpu_custom_call" | custom-call | tf_op jit(solution)/shard_map/pallas_call | solution.py:511
Async XLA Ops:
  0.6 1.0 copy-start
  1.7 0.7 copy-start.1

commit v7 on v6

--- a/solution.py
+++ b/solution.py
@@ -276,19 +276,6 @@
         lambda: unit_all.at[across, :], lambda: unit_all.at[across, :],
         lambda: p_send.at[1, 2], lambda: p_recv.at[1, 2], c_dev,
     ))
-    for i, p in enumerate(plane_from):
-        landed(cg_all.at[at(p, rows), :], p_recv.at[2, i])
-    landed(unit_all.at[at(q_c, rows), :], p_recv.at[1, 1])
-    landed(unit_all.at[at(q_d, rows), :], p_recv.at[1, 2])
-    cpart[...] = lax.dot_general(
-        cg_all[...], unit_all[...], (((0,), (0,)), ((), ())), preferred_element_type=jnp.float32
-    )
-    for i, t in enumerate(line):
-        send(None, remote(
-            lambda t=t: cpart.at[at(t, cz), :], lambda: cslots.at[z],
-            lambda i=i: c_send.at[i], lambda i=i: c_recv.at[i], {"dp": t * PLANE + q},
-        ))
-
     own_feat.wait()
     for i, p in enumerate(plane_from):
         theirs = at(p, rows)
@@ -392,6 +379,20 @@
 
         only(has(c, q_c), own)
         only(has(c, q_d), crossed)
+
+    def class_sums():
+        for i, p in enumerate(plane_from):
+            landed(cg_all.at[at(p, rows), :], p_recv.at[2, i])
+        landed(unit_all.at[at(q_c, rows), :], p_recv.at[1, 1])
+        landed(unit_all.at[at(q_d, rows), :], p_recv.at[1, 2])
+        cpart[...] = lax.dot_general(
+            cg_all[...], unit_all[...], (((0,), (0,)), ((), ())), preferred_element_type=jnp.float32
+        )
+        for i, t in enumerate(line):
+            send(None, remote(
+                lambda t=t: cpart.at[at(t, cz), :], lambda: cslots.at[z],
+                lambda i=i: c_send.at[i], lambda i=i: c_recv.at[i], {"dp": t * PLANE + q},
+            ))
 
     def class_rows():
         for i, t in enumerate(line_from):
@@ -428,22 +429,33 @@
         (0, multiply), (1, sum_near), (2, sum_far), (3, gather_far), (4, gather_near),
         (7, gather_across), (9, gather_core),
     )
+    starts, settled = [], [0]
+
+    def settle(end):
+        for cond, make in pending[settled[0]:end]:
+            only(cond, lambda: make().wait_send())
+        settled[0] = max(settled[0], end)
+
     for tick in range(count + stages[-1][0]):
         for late, run in stages:
             c = tick - late
             if 0 <= c < count:
                 run(c, pl.ds(*chunks[c]))
-        if tick == 3:
+        if tick == 2:
+            class_sums()
+        if tick == 5:
             class_rows()
-        if tick == 6:
+        if tick == 8:
             class_plane()
-        if tick == 9:
+        if tick == 11:
             class_across()
+        starts.append(len(pending))
+        if tick >= 5:
+            settle(starts[tick - 5])
 
     landed(cout.at[at(q_c, cq), :], cp_recv.at[1])
     landed(cout.at[at(q_d, cq), :], cp_recv.at[2])
-    for cond, make in pending:
-        only(cond, lambda: make().wait_send())
+    settle(len(pending))
 
 
 def place(chunks, per, *refs):

time: 107 us -> 112 us (1.047)
  Pallas kernels: 104 us -> 110 us
    pallas_call x1, Pallas kernels: 101 us -> 107 us  [fused(): pl.pallas_call(functools.partial(kernel, nz, chunks, rows * n_dp), out_sh...]
where the time goes in v7:
time: 112 us
  Pallas kernels  110 us (98%)
  local copies, waits for them, and re-layouts  1.69 us (2%)
    pallas_call x1, Pallas kernels, fused(): pl.pallas_call(functools.partial(kernel, nz, chunks, rows * n_dp), out_sh...  107 us
    pallas_call x1, Pallas kernels, fused(): pl.pallas_call(functools.partial(place, chunks, blocks // PLANE * LANES),...  3.11 us

profile of v7, /device:TPU:1, one launch (start us, length us, event | category | flops | bytes accessed | tf_op | source)
XLA Modules:
  0.0 112.0 jit_solution(14356396873342858747)
XLA Ops:
  0.6 0.0 copy-start
  0.6 1.0 copy-done
  1.7 0.0 copy-start.1
  1.7 0.7 copy-done.1
  2.3 106.5 %shard_map.59 = (bf16[4,4,128,128]{3,2,1,0:T(8,128)(2,1)S(1)}, bf16[4,4,256,128]{3,2,1,0:T(8,128)(2,1)S(1)}, bf16[4,4,256,128]{3,2,1,0:T(8,128)(2,1)S(1)}, bf16[...) custom-call(bf16[128,6272]{1,0:T(8,128)(2,1)} %feat_hbm.1, ...), custom_call_target="tpu_custom_call" | custom-call | tf_op jit(solution)/shard_map/pallas_call | solution.py:496
  108.9 3.1 %shard_map.60 = (bf16[6272,512]{1,0:T(8,128)(2,1)}, bf16[512,512]{1,0:T(8,128)(2,1)}) custom-call(bf16[4,4,128,128]{3,2,1,0:T(8,128)(2,1)S(1)} %get-tuple-element.11.refs_0_, bf16[4,4,256,128]{3,2,1,0:T(8,128)(2,1)S(1)} %get-tuple-element.12.refs_1_, bf16[4,4,256,128]{3,2,1,0:T(8,128)(2,1)S(1)} %get-tuple-element.13.refs_2_, ...), custom_call_target="tpu_custom_call" | custom-call | tf_op jit(solution)/shard_map/pallas_call | solution.py:523
Async XLA Ops:
  0.6 1.0 copy-start
  1.7 0.7 copy-start.1

commit v8 on v6

--- a/solution.py
+++ b/solution.py
@@ -264,10 +264,10 @@
     unit_grad = pgrad[...].astype(jnp.float32) + rgrad[...].astype(jnp.float32)
     along = jnp.sum(unit_f * unit_grad, axis=1, keepdims=True)
     rg_all[mine, :] = ((unit_grad - unit_f * along) / norm).astype(ROUNDED)
-    for i, p in enumerate(plane):
+    for i, dev in enumerate((y_dev, c_dev)):
         send(None, remote(
             lambda: rg_all.at[mine, :], lambda: rg_all.at[mine, :],
-            lambda i=i: p_send.at[3, i], lambda i=i: p_recv.at[3, i], {"dp": z * PLANE + p},
+            lambda i=i: p_send.at[3, i], lambda i=i: p_recv.at[3, i], dev,
         ))
 
     across = at(q_y, rows)
@@ -289,11 +289,16 @@
             lambda i=i: c_send.at[i], lambda i=i: c_recv.at[i], {"dp": t * PLANE + q},
         ))
 
+    landed(rg_all.at[across, :], p_recv.at[3, 0])
+    send(None, remote(
+        lambda: rg_all.at[across, :], lambda: rg_all.at[across, :],
+        lambda: p_send.at[3, 2], lambda: p_recv.at[3, 2], c_dev,
+    ))
     own_feat.wait()
     for i, p in enumerate(plane_from):
-        theirs = at(p, rows)
-        landed(gath.at[theirs, :], p_recv.at[0, i])
-        landed(rg_all.at[theirs, :], p_recv.at[3, i])
+        landed(gath.at[at(p, rows), :], p_recv.at[0, i])
+    landed(rg_all.at[at(q_c, rows), :], p_recv.at[3, 1])
+    landed(rg_all.at[at(q_d, rows), :], p_recv.at[3, 2])
 
     count = len(chunks)
 

time: 107 us -> 108 us (level)
  no operation moved by 1% of the time
where the time goes in v8:
time: 108 us; the launch traced here: 107 us
  Pallas kernels  105 us (97%)
  local copies, waits for them, and re-layouts  1.69 us (2%)
    pallas_call x1, Pallas kernels, fused(): pl.pallas_call(functools.partial(kernel, nz, chunks, rows * n_dp), out_sh...  102 us
    pallas_call x1, Pallas kernels, fused(): pl.pallas_call(functools.partial(place, chunks, blocks // PLANE * LANES),...  3.11 us

profile of v8, /device:TPU:1, one launch (start us, length us, event | category | flops | bytes accessed | tf_op | source)
XLA Modules:
  0.0 107.4 jit_solution(18134612941319115049)
XLA Ops:
  0.6 0.0 copy-start
  0.6 1.0 copy-done
  1.7 0.0 copy-start.1
  1.7 0.7 copy-done.1
  2.3 102.0 %shard_map.59 = (bf16[4,4,128,128]{3,2,1,0:T(8,128)(2,1)S(1)}, bf16[4,4,256,128]{3,2,1,0:T(8,128)(2,1)S(1)}, bf16[4,4,256,128]{3,2,1,0:T(8,128)(2,1)S(1)}, bf16[...) custom-call(bf16[128,6272]{1,0:T(8,128)(2,1)} %feat_hbm.1, ...), custom_call_target="tpu_custom_call" | custom-call | tf_op jit(solution)/shard_map/pallas_call | solution.py:489
  104.3 3.1 %shard_map.60 = (bf16[6272,512]{1,0:T(8,128)(2,1)}, bf16[512,512]{1,0:T(8,128)(2,1)}) custom-call(bf16[4,4,128,128]{3,2,1,0:T(8,128)(2,1)S(1)} %get-tuple-element.11.refs_0_, bf16[4,4,256,128]{3,2,1,0:T(8,128)(2,1)S(1)} %get-tuple-element.12.refs_1_, bf16[4,4,256,128]{3,2,1,0:T(8,128)(2,1)S(1)} %get-tuple-element.13.refs_2_, ...), custom_call_target="tpu_custom_call" | custom-call | tf_op jit(solution)/shard_map/pallas_call | solution.py:516
Async XLA Ops:
  0.6 1.0 copy-start
  1.7 0.7 copy-start.1

commit v9 on v6

--- a/solution.py
+++ b/solution.py
@@ -90,7 +90,7 @@
 
 
 def split_rows(blocks):
-    sizes = [1] + [2] * ((blocks - 1) // 2)
+    sizes = [1] + [3] * ((blocks - 2) // 3)
     sizes += [1] * (blocks - sum(sizes))
     return [(sum(sizes[:i]) * LANES, size * LANES) for i, size in enumerate(sizes)]
 

time: 107 us -> 109 us (1.019); the launches traced: 106 us -> 107 us
  no operation moved by 1% of the time
where the time goes in v9:
time: 109 us; the launch traced here: 107 us
  Pallas kernels  105 us (96%)
  local copies, waits for them, and re-layouts  1.69 us (2%)
    pallas_call x1, Pallas kernels, fused(): pl.pallas_call(functools.partial(kernel, nz, chunks, rows * n_dp), out_sh...  102 us
    pallas_call x1, Pallas kernels, fused(): pl.pallas_call(functools.partial(place, chunks, blocks // PLANE * LANES),...  3.07 us

profile of v9, /device:TPU:1, one launch (start us, length us, event | category | flops | bytes accessed | tf_op | source)
XLA Modules:
  0.0 107.3 jit_solution(3201311418708963948)
XLA Ops:
  0.6 0.0 copy-start
  0.6 1.0 copy-done
  1.7 0.0 copy-start.1
  1.7 0.7 copy-done.1
  2.3 101.9 %shard_map.59 = (bf16[4,4,128,128]{3,2,1,0:T(8,128)(2,1)S(1)}, bf16[4,4,384,128]{3,2,1,0:T(8,128)(2,1)S(1)}, bf16[4,4,384,128]{3,2,1,0:T(8,128)(2,1)S(1)}, bf16[...) custom-call(bf16[128,6272]{1,0:T(8,128)(2,1)} %feat_hbm.1, ...), custom_call_target="tpu_custom_call" | custom-call | tf_op jit(solution)/shard_map/pallas_call | solution.py:484
  104.3 3.1 %shard_map.60 = (bf16[6272,512]{1,0:T(8,128)(2,1)}, bf16[512,512]{1,0:T(8,128)(2,1)}) custom-call(bf16[4,4,128,128]{3,2,1,0:T(8,128)(2,1)S(1)} %get-tuple-element.10.refs_0_, bf16[4,4,384,128]{3,2,1,0:T(8,128)(2,1)S(1)} %get-tuple-element.11.refs_1_, bf16[4,4,384,128]{3,2,1,0:T(8,128)(2,1)S(1)} %get-tuple-element.12.refs_2_, ...), custom_call_target="tpu_custom_call" | custom-call | tf_op jit(solution)/shard_map/pallas_call | solution.py:511
Async XLA Ops:
  0.6 1.0 copy-start
  1.7 0.7 copy-start.1
